TPU v7x, 128 devices: a whole 4x4x4 slice. The times are simulated.
128 devices in a mesh: dp: 32 (over y, z, core), head: 4 (over x).
Axes of the slice: x: 4, y: 4, z: 4, core: 2. Of those that a mesh axis runs over, the one named last changes fastest.
Arguments:
- tokens: bfloat16 [32768, 768], P(('dp', 'head')), may hold values from -6 to 6
- cotangent: bfloat16 [32768, 768], P(('dp', 'head'))
- lengths: int32 [32], P('dp'), may hold values from 128 to 1024, as said below
- routes: int32 [32768, 1], P(('dp', 'head')), may hold values from 0 to 31; in each aligned block of 256 rows (0 to 255, 256 to 511, ...) at most 16 rows name the same one
- norms: float32 [4, 768], replicated
- w_qkv: float32 [3, 768, 768], P(None, None, 'head'), may hold values from -0.3125 to 0.3125
- w_out: float32 [768, 768], P('head'), may hold values from -0.875 to 0.875
- router: float32 [768, 32], replicated, may hold values from -0.15625 to 0.15625
- w_up: float32 [32, 768, 3072], P('dp', None, 'head')
- w_down: float32 [32, 3072, 768], P('dp', 'head'), may hold values from -0.3125 to 0.3125
- first_norms: float32 [4, 768], replicated, may hold values from -0.0009765625 to 0.0009765625
- second_norms: float32 [4, 768], replicated, may hold values from 2.0862959e-10 to 3.3380734e-09
- first_qkv: float32 [3, 768, 768], P(None, None, 'head'), may hold values from -0.00012207031 to 0.00012207031
- second_qkv: float32 [3, 768, 768], P(None, None, 'head'), may hold values from 3.2598373e-12 to 5.2157396e-11
- first_out: float32 [768, 768], P('head'), may hold values from -0.00012207031 to 0.00012207031
- second_out: float32 [768, 768], P('head'), may hold values from 3.2598373e-12 to 5.2157396e-11
- first_router: float32 [768, 32], replicated, may hold values from -0.00012207031 to 0.00012207031
- second_router: float32 [768, 32], replicated, may hold values from 3.2598373e-12 to 5.2157396e-11
- first_up: float32 [32, 768, 3072], P('dp', None, 'head'), may hold values from -0.00012207031 to 0.00012207031
- second_up: float32 [32, 768, 3072], P('dp', None, 'head'), may hold values from 3.2598373e-12 to 5.2157396e-11
- first_down: float32 [32, 3072, 768], P('dp', 'head'), may hold values from -0.00012207031 to 0.00012207031
- second_down: float32 [32, 3072, 768], P('dp', 'head'), may hold values from 3.2598373e-12 to 5.2157396e-11
Outputs:
- output: bfloat16 [32768, 768], P(('dp', 'head'))
- input_grad: float32 [32768, 768], P(('dp', 'head'))
- grad_norm: float32 [], replicated
- next_first_norms: float32 [4, 768], replicated
- next_second_norms: float32 [4, 768], replicated
- next_norms: float32 [4, 768], replicated
- next_first_qkv: float32 [3, 768, 768], P(None, None, 'head')
- next_second_qkv: float32 [3, 768, 768], P(None, None, 'head')
- next_qkv: float32 [3, 768, 768], P(None, None, 'head')
- next_first_out: float32 [768, 768], P('head')
- next_second_out: float32 [768, 768], P('head')
- next_out: float32 [768, 768], P('head')
- next_first_router: float32 [768, 32], replicated
- next_second_router: float32 [768, 32], replicated
- next_router: float32 [768, 32], replicated
- next_first_up: float32 [32, 768, 3072], P('dp', None, 'head')
- next_second_up: float32 [32, 768, 3072], P('dp', None, 'head')
- next_up: float32 [32, 768, 3072], P('dp', None, 'head')
- next_first_down: float32 [32, 3072, 768], P('dp', 'head')
- next_second_down: float32 [32, 3072, 768], P('dp', 'head')
- next_down: float32 [32, 3072, 768], P('dp', 'head')
Inputs may be any that keep to these rules, and one draw needn't show every extreme that they name: `lengths`: one sequence has length 1024; the others spread over the whole range. `routes`: at most 16 of the rows of one device name the same expert.
All inputs are finite; a program needn't handle non-finite values.
Results may differ from a plain program's by a relative error of at most 0.018.
The roundings to bfloat16 on the way count: a program that leaves them out, or rounds other values in their place, can miss the bound.
Values may be sent and summed in bfloat16 or wider, within the bound.
A program may use at most 192 MiB of HBM per device.

v0:
```python
import functools

import jax
import jax.numpy as jnp
from jax import lax
from jax.experimental import pallas as pl
from jax.experimental.pallas import tpu as pltpu
from jax.sharding import PartitionSpec as P

BF = jnp.bfloat16
F32 = jnp.float32
HD = 64
STEP = 10
PRECISE = lax.Precision.HIGHEST
EPS_NORM = 1e-05
BETA_ONE = 0.9
BETA_TWO = 0.999
ADAM_EPS = 1e-08
WEIGHT_DECAY = 0.01
CLIP_NORM = 1.0
NEGATIVE = -1e30
MESH = pl.DeviceIdType.MESH
N_HEAD = 4
N_DP = 32
N_CHIP = 16
CAP = 16
VM = pl.BlockSpec(memory_space=pltpu.VMEM)
SM = pl.BlockSpec(memory_space=pltpu.SMEM)
NT = (((1,), (1,)), ((), ()))
TN = (((0,), (0,)), ((), ()))


def dot(a, b, dims=(((1,), (0,)), ((), ())), precision=None):
    return lax.dot_general(a, b, dims, precision=precision, preferred_element_type=F32)


def cost(us):
    return pl.CostEstimate(
        flops=int(us * 1.1e9), bytes_accessed=int(us * 1e6), transcendentals=0
    )


def params(cid=None, vmem=48):
    if cid is None:
        return pltpu.CompilerParams(vmem_limit_bytes=vmem << 20)
    return pltpu.CompilerParams(
        collective_id=cid, has_side_effects=True, vmem_limit_bytes=vmem << 20
    )


def out(shape, dtype):
    return jax.ShapeDtypeStruct(shape, dtype)


def normed(values):
    average = jnp.mean(values, axis=-1, keepdims=True)
    centered = values - average
    variance = jnp.mean(centered * centered, axis=-1, keepdims=True)
    scale = lax.rsqrt(variance + EPS_NORM)
    return centered * scale, scale


def norm_back(grad, gain, xhat, scale):
    dxhat = grad * gain
    return scale * (
        dxhat
        - jnp.mean(dxhat, axis=-1, keepdims=True)
        - xhat * jnp.mean(dxhat * xhat, axis=-1, keepdims=True)
    )


def along_x(step):
    return lax.rem(lax.axis_index("head") + step, N_HEAD)


def remote(src, dst, sems, i, device):
    send, recv = sems
    return pltpu.make_async_remote_copy(
        src_ref=src,
        dst_ref=dst,
        send_sem=send.at[i],
        recv_sem=recv.at[i],
        device_id=device,
        device_id_type=MESH,
    )


def greet(devices):
    barrier = pltpu.get_barrier_semaphore()
    for device in devices:
        pl.semaphore_signal(barrier, inc=1, device_id=device, device_id_type=MESH)
    pl.semaphore_wait(barrier, len(devices))


def head_lanes(h):
    group = h // 2
    lane = lax.broadcasted_iota(jnp.int32, (1, 128), 1)
    mask = (lane // HD == h - 2 * group).astype(F32)
    return pl.ds(pl.multiple_of(group * 128, 128), 128), mask, lane


def kept(i, rows, keys, length):
    row = i * rows + lax.broadcasted_iota(jnp.int32, (rows, keys), 0)
    col = lax.broadcasted_iota(jnp.int32, (rows, keys), 1)
    return (col <= row) & (col < length)


def attend(length, qkv, o, lse):
    blocks, rows = o.shape[0], o.shape[1]
    o[...] = jnp.zeros_like(o)
    lse[...] = jnp.zeros_like(lse)

    def one_head(h, carry):
        lanes, mask, lane = head_lanes(h)
        q_mask = (mask * HD ** (-0.5)).astype(BF)
        for i in range(blocks):
            here = slice(i * rows, (i + 1) * rows)
            keys = (i + 1) * rows
            scores = dot(qkv[0, here, lanes] * q_mask, qkv[1, 0:keys, lanes], NT)
            scores = jnp.where(kept(i, rows, keys, length), scores, NEGATIVE)
            top = jnp.max(scores, axis=-1, keepdims=True)
            exponent = jnp.exp(scores - top)
            total = jnp.sum(exponent, axis=-1, keepdims=True)
            probs = (exponent * (1.0 / total)).astype(BF)
            result = dot(probs, qkv[2, 0:keys, lanes]) * mask
            o[i, :, lanes] = o[i, :, lanes] + result.astype(BF)
            lse[here, :] = lse[here, :] + jnp.where(lane == h, top + jnp.log(total), 0.0)
        return carry

    lax.fori_loop(0, 3, one_head, 0)


def attend_back(length, qkv, lse, grad_heads, grad_qkv, keys_sum, values_sum):
    blocks, rows = grad_heads.shape[0], grad_heads.shape[1]
    grad_qkv[...] = jnp.zeros_like(grad_qkv)
    keys_sum[...] = jnp.zeros_like(keys_sum)
    values_sum[...] = jnp.zeros_like(values_sum)

    def one_head(h, carry):
        lanes, mask, lane = head_lanes(h)
        scaled = (mask * HD ** (-0.5)).astype(BF)
        plain = mask.astype(BF)
        for i in range(blocks):
            here = slice(i * rows, (i + 1) * rows)
            keys = (i + 1) * rows
            q = qkv[0, here, lanes] * scaled
            k = qkv[1, 0:keys, lanes]
            grad = grad_heads[i, :, lanes] * plain
            scores = dot(q, k, NT)
            scores = jnp.where(kept(i, rows, keys, length), scores, NEGATIVE)
            level = jnp.sum(jnp.where(lane == h, lse[here, :], 0.0), axis=-1, keepdims=True)
            probs = jnp.exp(scores - level)
            grad_probs = dot(grad, qkv[2, 0:keys, lanes], NT)
            row_dot = jnp.sum(probs * grad_probs, axis=-1, keepdims=True)
            grad_scores = (probs * (grad_probs - row_dot)).astype(BF)
            grad_q = dot(grad_scores, k * scaled).astype(BF)
            grad_qkv[0, here, lanes] = grad_qkv[0, here, lanes] + grad_q
            keys_sum[0:keys, lanes] += dot(grad_scores, q, TN)
            values_sum[0:keys, lanes] += dot(probs.astype(BF), grad, TN)
        return carry

    lax.fori_loop(0, 3, one_head, 0)
    grad_qkv[1] = keys_sum[...].astype(BF)
    grad_qkv[2] = values_sum[...].astype(BF)


class Swap:
    def __init__(self, src, dst, relay, sems, first):
        me, right, across, left = (along_x(s) for s in range(4))
        half = src.shape[1] // 2
        top, low = pl.ds(0, half), pl.ds(half, half)
        to_right, to_left = {"head": right}, {"head": left}
        self.far = [
            remote(src.at[across, top], relay.at[0], sems, first, to_right),
            remote(src.at[across, low], relay.at[1], sems, first + 1, to_left),
        ]
        self.near = [
            remote(src.at[right], dst.at[me], sems, first + 2, to_right),
            remote(src.at[left], dst.at[me], sems, first + 3, to_left),
        ]
        self.onward = [
            remote(relay.at[0], dst.at[left, top], sems, first + 4, to_right),
            remote(relay.at[1], dst.at[right, low], sems, first + 5, to_left),
        ]

    def start(self):
        for c in self.far + self.near:
            c.start()

    def relay(self):
        for c, d in zip(self.far, self.onward):
            c.wait_recv()
            d.start()

    def wait(self):
        for c in self.far:
            c.wait_send()
        for c in self.near + self.onward:
            c.wait()


class Ring:
    def __init__(self, whole, part, sems, first):
        me, right, across, left = (along_x(s) for s in range(4))
        start, size = part
        half = size // 2
        top, low = pl.ds(start, half), pl.ds(start + half, half)

        def pass_on(block, part, i, device):
            ref = whole.at[block, part]
            return remote(ref, ref, sems, first + i, {"head": device})

        self.first = [
            pass_on(me, top, 0, right),
            pass_on(me, low, 1, left),
            pass_on(me, low, 2, right),
            pass_on(me, top, 3, left),
        ]
        self.onward = [pass_on(left, top, 4, right), pass_on(right, low, 5, left)]

    def start(self):
        for c in self.first:
            c.start()

    def relay(self):
        for c, d in zip(self.first[0:2], self.onward):
            c.wait_recv()
            d.start()

    def wait_send(self):
        for c in self.first + self.onward:
            c.wait_send()


def targets():
    steps = [(2, 2), (2, 1), (1, 2), (2, 3), (3, 2), (2, 0), (0, 2), (1, 1), (3, 3)]
    steps += [(1, 3), (3, 1), (1, 0), (0, 1), (3, 0), (0, 3), (0, 0)]
    return [(dy, dz, dc) for dc in (0, 1) for dy, dz in steps if (dy, dz, dc) != (0, 0, 0)]


def place_of(dp):
    return dp // 8, lax.rem(dp // 2, 4), lax.rem(dp, 2)


def dp_of(y, z, core):
    return lax.rem(y, 4) * 8 + lax.rem(z, 4) * 2 + lax.rem(core, 2)


def dp_peers():
    y, z, core = place_of(lax.axis_index("dp"))
    return [dp_of(y + dy, z + dz, core + dc) for dy, dz, dc in targets()]


def exchange(src, dst, sems, local):
    me = lax.axis_index("dp")
    copies = [
        remote(src.at[device], dst.at[me], sems, i, {"dp": device})
        for i, device in enumerate(dp_peers())
    ]
    copies.append(pltpu.make_async_copy(src.at[me], dst.at[me], local))
    return copies


def start(copies):
    for c in copies:
        c.start()


def wait(copies):
    for c in copies:
        c.wait()


def picks(routes_row, experts, rows):
    spread = jnp.broadcast_to(routes_row.astype(F32), (128, rows)).T
    lane = lax.broadcasted_iota(jnp.int32, (rows, experts), 1).astype(F32)
    return spread, (spread[:, 0:experts] == lane).astype(F32)


def dma(n):
    return [pltpu.SemaphoreType.DMA((n,)), pltpu.SemaphoreType.DMA((n,))]


X_PEERS = (1, 2, 3)
CHUNKS = 12
CHUNK = 128


def gelu_both(v):
    c = 0.7978845608028654
    square = v * v
    t = jnp.tanh(c * v * (1.0 + 0.044715 * square))
    half = 0.5 * (1.0 + t)
    slope = half + 0.5 * v * (1.0 - t * t) * (c * (1.0 + 3 * 0.044715 * square))
    return v * half, slope


def halves(ref):
    n, _, width = ref.shape
    sent = ref[:, 0:CAP, :].reshape(n * CAP, width)
    grad = ref[:, CAP : 2 * CAP, :].reshape(n * CAP, width)
    return sent, grad


def units(sent, grad, up, down):
    value, slope = gelu_both(dot(sent, up, NT))
    hidden = value.astype(BF)
    grad_pre = (dot(grad, down, NT) * slope).astype(BF)
    return hidden, grad_pre


TILE = 256
CHUNKS = 12
CHUNK = 128
ROW_CHUNKS = 8
HBM = pl.BlockSpec(memory_space=pltpu.HBM)


def counted_rows(length, rows):
    row = lax.axis_index("head") * rows + lax.broadcasted_iota(jnp.int32, (rows, 128), 0)
    return (row < length).astype(F32)[:, 0:1]


def add_rows(ref, w_own, grad_up, grad_down, first=False):
    def step(f, carry):
        here = pl.ds(pl.multiple_of(f * TILE, TILE), TILE)
        sent, grad = halves(ref)
        hidden, grad_pre = units(sent, grad, w_own[0, here, :], w_own[1, here, :])
        one_up = dot(sent, grad_pre, TN)
        one_down = dot(hidden, grad, TN)
        if first:
            grad_up[:, here] = one_up
            grad_down[here, :] = one_down
        else:
            grad_up[:, here] += one_up
            grad_down[here, :] += one_down
        return carry

    lax.fori_loop(0, 768 // TILE, step, 0)


class Copies:
    def __init__(self, sems):
        self.sems, self.started = sems, []

    def start(self, src, dst):
        c = pltpu.make_async_copy(src, dst, self.sems.at[len(self.started)])
        c.start()
        self.started.append(c)
        return c


def front_kernel(
    length_ref,
    norms,
    router,
    routes,
    tokens_in,
    cotangent_in,
    w_qkv,
    w_out,
    w_up,
    w_down,
    a_out,
    qkv_out,
    w_low_out,
    wo_out,
    o_out,
    lse_out,
    x_out,
    gates_out,
    place_out,
    w_out_low,
    returned,
    left_rows,
    right_rows,
    up_out,
    down_out,
    tokens,
    cotangent,
    wq_wide,
    wo_wide,
    up_wide,
    down_wide,
    a_full,
    qkv,
    w_low,
    wo_full,
    o,
    o_rows,
    o_relay,
    lse,
    x_one,
    gates_wide,
    place,
    slots,
    got,
    w_own,
    w_left,
    w_right,
    w_across,
    res,
    back,
    local,
    saved,
    a_send,
    a_recv,
    wo_send,
    wo_recv,
    o_send,
    o_recv,
    x_send,
    x_recv,
    w_send,
    w_recv,
    v_send,
    v_recv,
    r_send,
    r_recv,
    b_send,
    b_recv,
):
    me, right, across, left = (along_x(s) for s in range(4))
    to_right, to_left = {"head": right}, {"head": left}
    core = lax.rem(lax.axis_index("dp"), 2)
    partner = {"dp": lax.axis_index("dp") + 1 - 2 * core}
    rows = tokens.shape[0]
    experts = router.shape[0]
    loads, saves = Copies(local), Copies(saved)
    load_tokens = loads.start(tokens_in, tokens)
    load_qkv = loads.start(w_qkv, wq_wide)
    load_out = loads.start(w_out, wo_wide)
    load_up = loads.start(w_up, up_wide)
    load_down = loads.start(w_down, down_wide)
    load_cotangent = loads.start(cotangent_in, cotangent)
    load_tokens.wait()
    xhat, _ = normed(tokens[...].astype(F32))
    a_full[me] = (xhat * norms[0:1, :] + norms[1:2, :]).astype(BF)
    greet([{"head": along_x(s)} for s in X_PEERS] + [{"dp": d} for d in dp_peers()])
    ring = Ring(a_full, (0, rows), (a_send, a_recv), 0)
    ring.start()
    w_low[...] = jnp.zeros_like(w_low)
    load_qkv.wait()
    for c in range(3):
        w_low[256 * c : 256 * c + 192, :] = wq_wide[c].astype(BF)
    load_out.wait()
    wo_full[me] = wo_wide[...].astype(BF)

    def project(block):
        result = dot(a_full[block], w_low[...], NT).astype(BF)
        here = pl.ds(pl.multiple_of(block * rows, rows), rows)
        for c in range(3):
            qkv[c, here, :] = result[:, 256 * c : 256 * c + 256]

    project(me)
    ring.relay()
    mine = pl.multiple_of(core * 96, 96)
    wo_ring = Ring(wo_full, (mine, 96), (wo_send, wo_recv), 0)
    wo_ring.start()
    load_up.wait()
    w_own[0] = up_wide[...].T.astype(BF)
    load_down.wait()
    w_own[1] = down_wide[...].astype(BF)
    saves.start(w_own, w_out_low)
    saves.start(w_low, w_low_out)

    weights = []

    def send_weights(n):
        for k in range(len(weights) // 2, len(weights) // 2 + n):
            part = pl.ds((k // 2) * CHUNK, CHUNK)
            src = w_own.at[k % 2, part]
            sems = (w_send, w_recv)
            weights.append(remote(src, w_left.at[k % 2, part], sems, 2 * k, to_right))
            weights.append(remote(src, w_right.at[k % 2, part], sems, 2 * k + 1, to_left))
            weights[-2].start()
            weights[-1].start()

    ring.first[2].wait_recv()
    project(left)
    wo_ring.relay()
    send_weights(2)
    ring.first[3].wait_recv()
    project(right)
    for c in ring.onward:
        c.wait_recv()
    project(across)
    saves.start(a_full, a_out)
    saves.start(qkv, qkv_out)
    attend(length_ref[0], qkv, o, lse)
    saves.start(lse, lse_out)
    swap = Swap(o, o_rows, o_relay, (o_send, o_recv), 0)
    swap.start()
    for c in wo_ring.first[2:4] + wo_ring.onward:
        c.wait_recv()
    share = pl.ds(mine, 96)
    halves_over = []
    for i, block in enumerate((left, right, across)):
        ref = wo_full.at[block, share]
        halves_over.append(remote(ref, ref, (wo_send, wo_recv), 6 + i, partner))
    start(halves_over)
    o_rows[me] = o[me]
    spread, pick = picks(routes[...], experts, rows)
    row = lax.broadcasted_iota(jnp.int32, (rows, rows), 0)
    col = lax.broadcasted_iota(jnp.int32, (rows, rows), 1)
    earlier = dot((col < row).astype(BF), pick.astype(BF))
    slot = jnp.sum(earlier * pick, axis=-1, keepdims=True)
    target = spread[:, 0:1] * CAP + slot
    lane = lax.broadcasted_iota(jnp.int32, (rows, experts * CAP), 1).astype(F32)
    place[...] = (lane == target).astype(BF)
    saves.start(place, place_out)
    swap.relay()
    send_weights(2)
    wait(halves_over)
    saves.start(wo_full, wo_out)
    swap.wait()
    saves.start(o_rows, o_out)
    attention = dot(o_rows[0][:, 0:192], wo_full[0])
    for j in range(1, N_HEAD):
        attention = attention + dot(o_rows[j][:, 0:192], wo_full[j])
    x = tokens[...].astype(F32) + attention
    x_one[...] = x
    saves.start(x_one, x_out)
    xhat, _ = normed(x)
    h_two = xhat * norms[2:3, :] + norms[3:4, :]
    logits = dot(h_two, router[...], NT, PRECISE)
    gates = jax.nn.sigmoid(jnp.sum(logits * pick, axis=-1, keepdims=True))
    gates_wide[...] = jnp.broadcast_to(gates, gates_wide.shape)
    saves.start(gates_wide, gates_out)
    load_cotangent.wait()
    grad_out = cotangent[...].astype(F32) * counted_rows(length_ref[0], rows)
    to_slots = place[...]
    sent = dot(to_slots, h_two.astype(BF), TN).astype(BF)
    slots[:, 0:CAP, :] = sent.reshape(experts, CAP, -1)
    grad = dot(to_slots, (gates * grad_out).astype(BF), TN).astype(BF)
    slots[:, CAP : 2 * CAP, :] = grad.reshape(experts, CAP, -1)
    over = exchange(slots, got, (x_send, x_recv), local.at[6])
    start(over)
    send_weights(CHUNKS - 4)
    wait(over)

    onward = []

    def pass_weights(first, last):
        sems = (v_send, v_recv)
        for i in range(first, last):
            part = pl.ds(i * CHUNK, CHUNK)
            up = remote(w_left.at[0, part], w_across.at[0, part], sems, 2 * i, to_right)
            down = remote(
                w_right.at[1, part], w_across.at[1, part], sems, 2 * i + 1, to_left
            )
            weights[4 * i].wait_recv()
            up.start()
            weights[4 * i + 3].wait_recv()
            down.start()
            onward.extend((up, down))

    def add(w, f):
        here = pl.ds(pl.multiple_of(f * TILE, TILE), TILE)
        sent, grad = halves(got)
        hidden, grad_pre = units(sent, grad, w[0, here, :], w[1, here, :])
        res[...] += dot(hidden, w[1, here, :])
        back[...] += dot(grad_pre, w[0, here, :])

    def add_all(w):
        def step(f, carry):
            add(w, f)
            return carry

        lax.fori_loop(0, 768 // TILE, step, 0)

    res[...] = jnp.zeros_like(res)
    back[...] = jnp.zeros_like(back)
    pass_weights(0, 3)
    add_all(w_own)
    pass_weights(3, CHUNKS // 2)
    n = got.shape[0]
    round_rows = []
    for k in range(ROW_CHUNKS):
        part = pl.ds(k * (n // ROW_CHUNKS), n // ROW_CHUNKS)
        sems = (r_send, r_recv)
        round_rows.append(remote(got.at[part], left_rows.at[part], sems, 2 * k, to_right))
        round_rows.append(
            remote(got.at[part], right_rows.at[part], sems, 2 * k + 1, to_left)
        )
    start(round_rows)
    for i in range(CHUNKS // 2):
        weights[4 * i + 1].wait_recv()
        weights[4 * i + 2].wait_recv()
    add_all(w_left)
    add_all(w_right)
    for f in range(768 // TILE):
        for c in onward[4 * f : 4 * f + 4]:
            c.wait_recv()
        add(w_across, f)
    slots[:, 0:CAP, :] = res[...].astype(BF).reshape(n, CAP, -1)
    slots[:, CAP : 2 * CAP, :] = back[...].astype(BF).reshape(n, CAP, -1)
    over = exchange(slots, returned, (b_send, b_recv), local.at[7])
    start(over)
    add_rows(got, w_own, up_wide, down_wide, True)
    saves.start(up_wide, up_out)
    saves.start(down_wide, down_out)
    wait(over)
    wait(round_rows)
    for c in weights + onward:
        c.wait_send()
    ring.wait_send()
    wo_ring.wait_send()
    wait(saves.started)


def front(*args):
    rows, width = args[4].shape
    experts = args[2].shape[0]
    slots = (experts, 2 * CAP, width)
    outs = (
        out((N_HEAD, rows, width), BF),
        out((3, N_HEAD * rows, 256), BF),
        out((768, width), BF),
        out((N_HEAD, 192, width), BF),
        out((N_HEAD, rows, 256), BF),
        out((N_HEAD * rows, 128), F32),
        out((rows, width), F32),
        out((rows, 128), F32),
        out((rows, experts * CAP), BF),
        out((2, 768, width), BF),
        out(slots, BF),
        out(slots, BF),
        out(slots, BF),
        out((width, 768), F32),
        out((768, width), F32),
    )
    return pl.pallas_call(
        front_kernel,
        out_shape=outs,
        in_specs=[SM, VM, VM, VM] + [HBM] * 6,
        out_specs=(HBM,) * len(outs),
        scratch_shapes=[
            pltpu.VMEM((rows, width), BF),
            pltpu.VMEM((rows, width), BF),
            pltpu.VMEM((3, 192, width), F32),
            pltpu.VMEM((192, width), F32),
            pltpu.VMEM((width, 768), F32),
            pltpu.VMEM((768, width), F32),
            pltpu.VMEM((N_HEAD, rows, width), BF),
            pltpu.VMEM((3, N_HEAD * rows, 256), BF),
            pltpu.VMEM((768, width), BF),
            pltpu.VMEM((N_HEAD, 192, width), BF),
            pltpu.VMEM((N_HEAD, rows, 256), BF),
            pltpu.VMEM((N_HEAD, rows, 256), BF),
            pltpu.VMEM((2, rows // 2, 256), BF),
            pltpu.VMEM((N_HEAD * rows, 128), F32),
            pltpu.VMEM((rows, width), F32),
            pltpu.VMEM((rows, 128), F32),
            pltpu.VMEM((rows, experts * CAP), BF),
            pltpu.VMEM(slots, BF),
            pltpu.VMEM(slots, BF),
            *[pltpu.VMEM((2, 768, width), BF)] * 4,
            *[pltpu.VMEM((experts * CAP, width), F32)] * 2,
            pltpu.SemaphoreType.DMA((8,)),
            pltpu.SemaphoreType.DMA((12,)),
            *dma(6),
            *dma(9),
            *dma(6),
            *dma(N_DP - 1),
            *dma(2 * CHUNKS),
            *dma(CHUNKS),
            *dma(2 * ROW_CHUNKS),
            *dma(N_DP - 1),
        ],
        compiler_params=params(1, 62),
        cost_estimate=cost(130),
        name="front",
    )(*args)


def sum_squares(v):
    return jnp.sum(jnp.sum(v * v, axis=0, keepdims=True), axis=1, keepdims=True)


class RingSum:
    def __init__(self, far, near, from_far, from_near, sems, first):
        self.right, self.across, self.left = along_x(1), along_x(2), along_x(3)
        half = far.shape[0] // 2
        self.half, self.far, self.near = half, far, near
        self.from_far, self.from_near = from_far, from_near
        to_right, to_left = {"head": self.right}, {"head": self.left}
        top, low = pl.ds(0, half), pl.ds(half, half)
        self.one = remote(far.at[top], from_far.at[0], sems, first, to_right)
        self.two = remote(far.at[low], from_far.at[1], sems, first + 1, to_left)
        self.three = remote(near.at[0], from_near.at[0], sems, first + 2, to_right)
        self.four = remote(near.at[1], from_near.at[1], sems, first + 3, to_left)

    def send_far(self, value):
        self.far[...] = value.astype(BF)
        self.one.start()
        self.two.start()

    def send_near(self, for_right, for_left):
        h = self.half
        self.near[0, h:, :] = for_right[h:, :].astype(BF)
        self.near[1, 0:h, :] = for_left[0:h, :].astype(BF)
        self.one.wait_recv()
        self.near[0, 0:h, :] = (for_right[0:h, :] + self.from_far[0].astype(F32)).astype(BF)
        self.three.start()
        self.two.wait_recv()
        self.near[1, h:, :] = (for_left[h:, :] + self.from_far[1].astype(F32)).astype(BF)
        self.four.start()

    def arrived(self):
        self.three.wait_recv()
        self.four.wait_recv()
        return self.from_near[0].astype(F32) + self.from_near[1].astype(F32)

    def wait_send(self):
        for c in (self.one, self.two, self.three, self.four):
            c.wait_send()


HALF = 384
BLOCK = 48
LATER = 8


def back_kernel(
    length_ref,
    norms,
    router,
    routes,
    returned_in,
    place_in,
    gates_wide_in,
    x_in,
    cotangent_in,
    wo_in,
    o_in,
    left_in,
    w_own_in,
    up_in,
    down_in,
    qkv_in,
    lse_in,
    w_low_in,
    a_in,
    right_in,
    tokens_in,
    output_out,
    input_out,
    grad_out_w,
    small_out,
    norm_out,
    up_out,
    down_out,
    output,
    input_grad,
    grad_up,
    grad_down,
    returned,
    place,
    gates_in,
    x_one,
    cotangent,
    wo_full,
    o_rows,
    left_rows,
    w_own,
    qkv,
    lse,
    w_low,
    a_full,
    right_rows,
    tokens,
    across_rows,
    to_heads,
    grad_heads,
    relay,
    keys_sum,
    values_sum,
    grad_qkv,
    grad_x_one,
    far,
    near,
    from_far,
    from_near,
    out_far,
    out_near,
    out_from_far,
    out_from_near,
    out_cross,
    out_cross_in,
    out_sum,
    cross,
    cross_in,
    mine,
    low_mine,
    pieces,
    small,
    small_peer,
    tile_mine,
    tiles,
    tiles_x,
    whole,
    every,
    o_send,
    o_recv,
    r_send,
    r_recv,
    h_send,
    h_recv,
    c_send,
    c_recv,
    y_send,
    y_recv,
    local,
    saved,
):
    loads, saves = Copies(local), Copies(saved)
    first_loads = [
        loads.start(src, dst)
        for src, dst in (
            (returned_in, returned),
            (place_in, place),
            (gates_wide_in, gates_in),
            (x_in, x_one),
            (cotangent_in, cotangent),
            (wo_in, wo_full),
        )
    ]
    load_o = loads.start(o_in, o_rows)
    rows_loads = [
        loads.start(src, dst)
        for src, dst in (
            (left_in, left_rows),
            (w_own_in, w_own),
            (up_in, grad_up),
            (down_in, grad_down),
        )
    ]
    heads_loads = [loads.start(qkv_in, qkv), loads.start(lse_in, lse)]
    later_loads = [
        loads.start(src, dst)
        for src, dst in ((w_low_in, w_low), (a_in, a_full), (right_in, right_rows))
    ]
    load_tokens = loads.start(tokens_in, tokens)
    me, right, across, left = (along_x(s) for s in range(4))
    to_right, to_left = {"head": right}, {"head": left}
    dp = lax.axis_index("dp")
    y, z, core = place_of(dp)
    chip = dp // 2
    partner = {"dp": dp + 1 - 2 * core}
    steps = [(dy, dz) for dy, dz, dc in targets() if dc == 0]
    chips = [lax.rem(y + dy, 4) * 4 + lax.rem(z + dz, 4) for dy, dz in steps]
    peers = [{"dp": 2 * t + core} for t in chips]
    others = [{"head": along_x(s)} for s in (2, 1, 3)]
    greet([partner] + peers + others)
    rows, width = x_one.shape
    experts = router.shape[0]
    n = left_in.shape[0]
    size = n // (2 * LATER)
    later = []
    sems = (r_send, r_recv)
    for k in range(LATER):
        top, low = pl.ds(k * size, size), pl.ds(n // 2 + k * size, size)
        later.append(remote(left_in.at[top], across_rows.at[top], sems, 2 * k, to_right))
        later.append(
            remote(right_in.at[low], across_rows.at[low], sems, 2 * k + 1, to_left)
        )
    start(later[0:4])
    wait(first_loads)

    to_slots = place[...]
    result, grad_sent = halves(returned)
    combined = dot(to_slots, result)
    gates = gates_in[:, 0:1]
    x = x_one[...]
    grad_out = cotangent[...].astype(F32) * counted_rows(length_ref[0], rows)
    grad_logit = jnp.sum(grad_out * combined, axis=-1, keepdims=True) * gates * (1.0 - gates)
    _, pick = picks(routes[...], experts, rows)
    columns = pick * grad_logit
    grad_h = dot(to_slots, grad_sent) + dot(columns, router[...], precision=PRECISE)
    xhat, scale = normed(x)
    gain = norms[2:3, :]
    grad_x = grad_out + norm_back(grad_h, gain, xhat, scale)
    low = grad_x.astype(BF)
    to_heads[:, :, 192:256] = jnp.zeros((N_HEAD, rows, 64), BF)
    for j in range(N_HEAD):
        to_heads[j, :, 0:192] = dot(low, wo_full[j], NT).astype(BF)
    swap = Swap(to_heads, grad_heads, relay, (o_send, o_recv), 0)
    swap.start()
    grad_heads[me] = to_heads[me]
    grad_x_one[...] = grad_x
    output[...] = (x + gates * combined).astype(BF)
    saves.start(output, output_out)

    theirs = pl.ds(pl.multiple_of((1 - core) * HALF, 128), HALF)
    ours = pl.ds(pl.multiple_of(core * HALF, 128), HALF)
    load_o.wait()
    for j in range(N_HEAD):
        out_sum[j] = dot(o_rows[j][:, 0:192], low, TN)
    swap.relay()
    start(later[4:])
    out_cross[...] = out_sum[:, :, theirs].astype(BF)
    joined = remote(out_cross, out_cross_in, (c_send, c_recv), 0, partner)
    joined.start()
    small[...] = jnp.zeros_like(small)
    small[2:3, :] = jnp.sum(grad_h * xhat, axis=0, keepdims=True)
    small[3:4, :] = jnp.sum(grad_h, axis=0, keepdims=True)
    h_two = xhat * gain + norms[3:4, :]
    small[8 : 8 + experts, :] = dot(columns, h_two, TN, PRECISE)

    joined.wait_recv()

    def out_block(block):
        return out_sum[block, :, ours] + out_cross_in[block].astype(F32)

    out_ring = RingSum(
        out_far, out_near, out_from_far, out_from_near, (h_send, h_recv), 4
    )
    out_ring.send_far(out_block(across))
    wait(rows_loads)
    add_rows(left_rows, w_own, grad_up, grad_down)
    swap.wait()
    wait(heads_loads)

    attend_back(length_ref[0], qkv, lse, grad_heads, grad_qkv, keys_sum, values_sum)

    wait(later_loads)

    def partial(block):
        here = pl.ds(pl.multiple_of(block * rows, rows), rows)
        total = dot(grad_qkv[0, here, :], w_low[0:256, :])
        total = total + dot(grad_qkv[1, here, :], w_low[256:512, :])
        return total + dot(grad_qkv[2, here, :], w_low[512:768, :])

    in_ring = RingSum(far, near, from_far, from_near, (h_send, h_recv), 0)
    in_ring.send_far(partial(across))
    out_ring.send_near(out_block(right), out_block(left))
    out_own = out_block(me)
    for c in range(3):
        total = dot(grad_qkv[c, 0:rows, :], a_full[0], TN)
        for j in range(1, N_HEAD):
            here = slice(j * rows, (j + 1) * rows)
            total = total + dot(grad_qkv[c, here, :], a_full[j], TN)
        out_sum[c] = total[0:192, :]
    cross[...] = out_sum[0:3, :, theirs].astype(BF)
    crossed = remote(cross, cross_in, (c_send, c_recv), 1, partner)
    crossed.start()
    in_ring.send_near(partial(right), partial(left))
    grad_in = partial(me)
    mine[576:768, :] = out_own + out_ring.arrived()
    crossed.wait_recv()
    for c in range(3):
        here = slice(192 * c, 192 * c + 192)
        mine[here, :] = out_sum[c, :, ours] + cross_in[c].astype(F32)
    low_mine[...] = mine[...].astype(BF)
    sems = (y_send, y_recv)
    base = 0
    many = len(steps)
    sums = []
    for i, t in enumerate(chips):
        src = low_mine.at[pl.ds(pl.multiple_of(t * BLOCK, BLOCK), BLOCK)]
        sums.append(remote(src, pieces.at[i], sems, base + i, peers[i]))
    start(sums)
    base += many

    add_rows(right_rows, w_own, grad_up, grad_down)
    load_tokens.wait()
    grad_in = grad_in + in_ring.arrived()
    xhat, scale = normed(tokens[...].astype(F32))
    input_grad[...] = grad_x_one[...] + norm_back(grad_in, norms[0:1, :], xhat, scale)
    saves.start(input_grad, input_out)
    small[0:1, :] = jnp.sum(grad_in * xhat, axis=0, keepdims=True)
    small[1:2, :] = jnp.sum(grad_in, axis=0, keepdims=True)
    over_small = remote(small.at[:, theirs], small_peer, (c_send, c_recv), 2, partner)
    over_small.start()

    for c in sums:
        c.wait_recv()
    here = pl.ds(pl.multiple_of(chip * BLOCK, BLOCK), BLOCK)
    piece = mine[here, :]
    for i in range(many):
        piece = piece + pieces[i].astype(F32)
    whole[core, here, :] = piece.astype(BF)
    gathers = []
    for i in range(many):
        ref = whole.at[core, here]
        gathers.append(remote(ref, ref, sems, base + i, peers[i]))
    start(gathers)
    base += many
    over_small.wait_recv()
    for t in range(15):
        r, l = 8 * (t // 3), 128 * (t % 3)
        where = pl.ds(pl.multiple_of(core * HALF + l, 128), 128)
        tile_mine[t] = small[r : r + 8, where] + small_peer[r : r + 8, l : l + 128]
    tile_mine[15] = jnp.zeros((8, 128), F32)
    tile_sums = []
    for i, t in enumerate(chips):
        tile_sums.append(remote(tile_mine.at[t], tiles.at[i], sems, base + i, peers[i]))
    start(tile_sums)
    base += many
    wait(later)
    add_rows(across_rows, w_own, grad_up, grad_down)
    saves.start(grad_up, up_out)
    saves.start(grad_down, down_out)
    squares = sum_squares(grad_up[...]) + sum_squares(grad_down[...]) + sum_squares(piece)
    for c in tile_sums:
        c.wait_recv()
    tile = tile_mine[chip]
    for i in range(many):
        tile = tile + tiles[i]
    tiles_x[me, 0] = tile
    tiles_x[me, 1] = jnp.broadcast_to(squares, (8, 128))
    swaps = []
    for i, device in enumerate(others):
        ref = tiles_x.at[me]
        swaps.append(remote(ref, ref, sems, base + i, device))
    start(swaps)
    base += 3
    for c in gathers:
        c.wait_recv()
    last = remote(whole.at[core], whole.at[core], sems, base, partner)
    last.start()
    base += 1
    for c in swaps:
        c.wait_recv()
    tile = (tiles_x[0, 0] + tiles_x[1, 0]) + (tiles_x[2, 0] + tiles_x[3, 0])
    score = (tiles_x[0, 1] + tiles_x[1, 1]) + (tiles_x[2, 1] + tiles_x[3, 1])
    every[core, chip, 0] = tile
    every[core, chip, 1] = score + jnp.broadcast_to(sum_squares(tile), (8, 128))
    spreads = []
    for i in range(many):
        ref = every.at[core, chip]
        spreads.append(remote(ref, ref, sems, base + i, peers[i]))
    start(spreads)
    base += many
    last.wait_recv()
    grad_out_w[:, 0:HALF] = whole[0]
    grad_out_w[:, HALF : 2 * HALF] = whole[1]
    for c in spreads:
        c.wait_recv()
    last_small = remote(every.at[core], every.at[core], sems, base, partner)
    last_small.start()
    last_small.wait_recv()
    total = every[0, 0, 1]
    for c in range(2):
        for t in range(N_CHIP):
            if c + t:
                total = total + every[c, t, 1]
            if t < 15:
                r, l = 8 * (t // 3), 128 * (t % 3)
                small_out[r : r + 8, HALF * c + l : HALF * c + l + 128] = every[c, t, 0]
    norm_out[...] = jnp.sqrt(total)
    out_ring.wait_send()
    in_ring.wait_send()
    for c in [joined, crossed, over_small, last, last_small]:
        c.wait_send()
    for c in sums + gathers + tile_sums + swaps + spreads:
        c.wait_send()
    wait(saves.started)


def back(*args):
    rows, width = args[7].shape
    slots = args[4].shape
    qkv = args[15].shape
    many = N_CHIP - 1
    return pl.pallas_call(
        back_kernel,
        out_shape=(
            out((rows, width), BF),
            out((rows, width), F32),
            out((768, width), BF),
            out((40, width), F32),
            out((8, 128), F32),
            out((width, 768), F32),
            out((768, width), F32),
        ),
        in_specs=[SM, VM, VM, VM] + [HBM] * 17,
        out_specs=(HBM, HBM, VM, VM, VM, HBM, HBM),
        scratch_shapes=[
            pltpu.VMEM((rows, width), BF),
            pltpu.VMEM((rows, width), F32),
            pltpu.VMEM((width, 768), F32),
            pltpu.VMEM((768, width), F32),
            *[pltpu.VMEM(v.shape, v.dtype) for v in args[4:13]],
            *[pltpu.VMEM(v.shape, v.dtype) for v in args[15:21]],
            pltpu.VMEM(slots, BF),
            pltpu.VMEM((N_HEAD, rows, 256), BF),
            pltpu.VMEM((N_HEAD, rows, 256), BF),
            pltpu.VMEM((2, rows // 2, 256), BF),
            pltpu.VMEM((qkv[1], 256), F32),
            pltpu.VMEM((qkv[1], 256), F32),
            pltpu.VMEM(qkv, BF),
            pltpu.VMEM((rows, width), F32),
            pltpu.VMEM((rows, width), BF),
            pltpu.VMEM((2, rows, width), BF),
            pltpu.VMEM((2, rows // 2, width), BF),
            pltpu.VMEM((2, rows, width), BF),
            pltpu.VMEM((192, HALF), BF),
            pltpu.VMEM((2, 192, HALF), BF),
            pltpu.VMEM((2, 96, HALF), BF),
            pltpu.VMEM((2, 192, HALF), BF),
            pltpu.VMEM((N_HEAD, 192, HALF), BF),
            pltpu.VMEM((N_HEAD, 192, HALF), BF),
            pltpu.VMEM((N_HEAD, 192, width), F32),
            pltpu.VMEM((3, 192, HALF), BF),
            pltpu.VMEM((3, 192, HALF), BF),
            pltpu.VMEM((768, HALF), F32),
            pltpu.VMEM((768, HALF), BF),
            pltpu.VMEM((many, BLOCK, HALF), BF),
            pltpu.VMEM((40, width), F32),
            pltpu.VMEM((40, HALF), F32),
            pltpu.VMEM((N_CHIP, 8, 128), F32),
            pltpu.VMEM((many, 8, 128), F32),
            pltpu.VMEM((N_HEAD, 2, 8, 128), F32),
            pltpu.VMEM((2, 768, HALF), BF),
            pltpu.VMEM((2, N_CHIP, 2, 8, 128), F32),
            *dma(6),
            *dma(2 * LATER),
            *dma(8),
            *dma(3),
            *dma(4 * many + 5),
            pltpu.SemaphoreType.DMA((18,)),
            pltpu.SemaphoreType.DMA((4,)),
        ],
        compiler_params=params(3, 58),
        cost_estimate=cost(60),
        name="back",
    )(*args)


def adam_step(gradient, moment_one, moment_two, weight, step_rate):
    first_new = BETA_ONE * moment_one + (1.0 - BETA_ONE) * gradient
    second_new = BETA_TWO * moment_two + (1.0 - BETA_TWO) * gradient * gradient
    first_hat = first_new / (1.0 - BETA_ONE**STEP)
    second_hat = second_new / (1.0 - BETA_TWO**STEP)
    weight_new = weight - step_rate * (
        first_hat / (jnp.sqrt(second_hat) + ADAM_EPS) + WEIGHT_DECAY * weight
    )
    return (first_new, second_new, weight_new)


RATES = (0.1, 0.5, 0.08, 0.1, 1.0, 0.05)
ADAM_STEPS = 6


def adam_kernel(norm, attn, small, output, input_grad, up, down, *refs):
    factor = jnp.minimum(1.0, CLIP_NORM / (norm[0:1, 0:1] + 1e-06))
    moments, results, norm_out = refs[0:18], refs[18:38], refs[38]
    results[18][...] = output[...]
    results[19][...] = input_grad[...]
    norm_out[0] = jnp.max(norm[...])
    step = pl.program_id(0)
    first, second = up.shape[0] * 3 // 4, up.shape[0] // 4
    grads = (
        attn[pl.ds(pl.multiple_of(step * first, 32), first), :],
        attn[pl.ds(pl.multiple_of(576 + step * second, 32), second), :],
        up[...],
        down[...],
        small[0:4, :],
        small[8:40, :],
    )

    def update(i):
        one, two, weight = (r[...] for r in moments[3 * i : 3 * i + 3])
        new = adam_step(grads[i].astype(F32) * factor, one, two, weight, RATES[i])
        for ref, value in zip(results[3 * i : 3 * i + 3], new):
            ref[...] = value

    for i in range(4):
        update(i)

    @pl.when(step == 0)
    def _():
        update(4)
        update(5)


def adam(norm, attn, small, output, input_grad, up, down, moments):
    def whole(v):
        return pl.BlockSpec(v.shape, lambda i: (0, 0))

    def tiled(v):
        return pl.BlockSpec((v.shape[0] // ADAM_STEPS, v.shape[1]), lambda i: (i, 0))

    def quarter(v):
        return pl.BlockSpec((v.shape[0] // 4, v.shape[1]), lambda i: (jnp.minimum(i, 3), 0))

    specs = [tiled(v) for v in moments[0:12]] + [whole(v) for v in moments[12:18]]
    rows = [quarter(output), quarter(input_grad)]
    return pl.pallas_call(
        adam_kernel,
        grid=(ADAM_STEPS,),
        out_shape=[out(v.shape, v.dtype) for v in (*moments, output, input_grad)]
        + [out((1,), F32)],
        in_specs=[whole(norm), whole(attn), whole(small)]
        + rows
        + [tiled(up), tiled(down)]
        + specs,
        out_specs=specs + rows + [SM],
        compiler_params=params(None, 58),
        cost_estimate=cost(13),
        name="adamw",
    )(norm, attn, small, output, input_grad, up, down, *moments)


def swapped(v):
    return jnp.swapaxes(v, -1, -2)


def per_device(
    tokens,
    cotangent,
    lengths,
    routes,
    norms,
    w_qkv,
    w_out,
    router,
    w_up,
    w_down,
    first_norms,
    second_norms,
    first_qkv,
    second_qkv,
    first_out,
    second_out,
    first_router,
    second_router,
    first_up,
    second_up,
    first_down,
    second_down,
):
    routes_row = routes.reshape(1, -1)
    router_t = swapped(router)
    (
        a_full,
        qkv,
        w_low,
        wo_full,
        o_rows,
        lse,
        x_one,
        gates,
        place,
        w_own,
        returned,
        left_rows,
        right_rows,
        part_up,
        part_down,
    ) = front(
        lengths,
        norms,
        router_t,
        routes_row,
        tokens,
        cotangent,
        swapped(w_qkv),
        w_out,
        w_up[0],
        w_down[0],
    )
    output, input_grad, grad_attn, small, norm, grad_up, grad_down = back(
        lengths,
        norms,
        router_t,
        routes_row,
        returned,
        place,
        gates,
        x_one,
        cotangent,
        wo_full,
        o_rows,
        left_rows,
        w_own,
        part_up,
        part_down,
        qkv,
        lse,
        w_low,
        a_full,
        right_rows,
        tokens,
    )

    def flat(v):
        return swapped(v).reshape(576, -1)

    moments = [flat(v) for v in (first_qkv, second_qkv, w_qkv)]
    moments += [first_out, second_out, w_out]
    moments += [v[0] for v in (first_up, second_up, w_up, first_down, second_down, w_down)]
    moments += [first_norms, second_norms, norms]
    moments += [swapped(v) for v in (first_router, second_router, router)]
    new = adam(norm, grad_attn, small, output, input_grad, grad_up, grad_down, moments)
    return (
        new[18],
        new[19],
        new[20].reshape(()),
        *new[12:15],
        *(swapped(v.reshape(3, 192, -1)) for v in new[0:3]),
        *new[3:6],
        *(swapped(v) for v in new[15:18]),
        *(v[None] for v in new[6:12]),
    )


def solution(mesh):
    both = ("dp", "head")
    by_row = P(both, None)
    qkv = P(None, None, "head")
    wo = P("head", None)
    up = P("dp", None, "head")
    down = P("dp", "head", None)
    in_specs = (
        (by_row, by_row, P("dp"), by_row, P(), qkv, wo, P(), up, down)
        + (P(), P(), qkv, qkv, wo, wo, P(), P(), up, up, down, down)
    )
    out_specs = (
        (by_row, by_row, P()) + (P(),) * 3 + (qkv,) * 3 + (wo,) * 3 + (P(),) * 3
        + (up,) * 3 + (down,) * 3
    )
    return jax.shard_map(
        per_device, mesh=mesh, in_specs=in_specs, out_specs=out_specs, check_vma=False
    )
```

profile of v0, /device:TPU:1, one launch (start us, length us, event | category | flops | bytes accessed | tf_op | source)
XLA Modules:
  0.0 245.0 jit_solution(7572809899577007824)
XLA Ops:
  1.3 148.2 %front.1 = (bf16[4,256,768]{2,1,0:T(8,128)(2,1)}, bf16[3,1024,256]{2,1,0:T(8,128)(2,1)}, bf16[768,768]{1,0:T(8,128)(2,1)}, bf16[4,192,768]{2,1,0:T(8,128)(2,1)},...) custom-call(s32[1]{0:T(128)S(6)} %copy.43.length_ref, ...), custom_call_target="tpu_custom_call" | custom-call | flops 142999994368 | bytes 130000000 | tf_op jit(solution)/shard_map/front/pallas_call | solution.py:633
  149.5 72.7 %back.1 = (bf16[256,768]{1,0:T(8,128)(2,1)}, f32[256,768]{1,0:T(8,128)}, bf16[768,768]{1,0:T(8,128)(2,1)}, f32[40,768]{1,0:T(8,128)}, f32[8,128]{1,0:T(8,128)}, /*index=5*/f32[768,768]{1,0:T(8,128)}, f32[768,768]{1,0:T(8,128)}) custom-call(s32[1]{0:T(128)S(6)} %copy.43.length_ref, f32[4,768]{1,0:T(4,128)} %refs_14_.1, f32[32,768]{1,0:T(8,128)} %bitcast.51, ...), custom_call_target="tpu_custom_call" | custom-call | flops 65999998976 | bytes 60000000 | tf_op jit(solution)/shard_map/back/pallas_call | solution.py:1067
  222.1 22.7 %adamw.1 = (f32[576,768]{1,0:T(8,128)}, f32[576,768]{1,0:T(8,128)}, f32[576,768]{1,0:T(8,128)}, f32[192,768]{1,0:T(8,128)}, f32[192,768]{1,0:T(8,128)}, /*index=...) custom-call(f32[8,128]{1,0:T(8,128)} %get-tuple-element.79.norm, ...), custom_call_target="tpu_custom_call" | custom-call | flops 14300000256 | bytes 13000000 | tf_op jit(solution)/shard_map/adamw/pallas_call | solution.py:1191
where the time goes:
time: 245 us
  Pallas kernels  244 us (100%)
    pallas_call x1, Pallas kernels, front(): pl.pallas_call(front_kernel, out_shape=outs, in_specs=[SM, VM, VM, VM] +...  148 us
    pallas_call x1, Pallas kernels, back(): pl.pallas_call(back_kernel, out_shape=(out((rows, width), BF), out((rows,...  72.7 us
    pallas_call x1, Pallas kernels, adam(): pl.pallas_call(adam_kernel, grid=(ADAM_STEPS,), out_shape=[out(v.shape, v...  22.7 us

commit v1 on v0

--- a/solution.py
+++ b/solution.py
@@ -165,38 +165,20 @@
 
 
 class Swap:
-    def __init__(self, src, dst, relay, sems, first):
-        me, right, across, left = (along_x(s) for s in range(4))
-        half = src.shape[1] // 2
-        top, low = pl.ds(0, half), pl.ds(half, half)
-        to_right, to_left = {"head": right}, {"head": left}
-        self.far = [
-            remote(src.at[across, top], relay.at[0], sems, first, to_right),
-            remote(src.at[across, low], relay.at[1], sems, first + 1, to_left),
-        ]
-        self.near = [
-            remote(src.at[right], dst.at[me], sems, first + 2, to_right),
-            remote(src.at[left], dst.at[me], sems, first + 3, to_left),
-        ]
-        self.onward = [
-            remote(relay.at[0], dst.at[left, top], sems, first + 4, to_right),
-            remote(relay.at[1], dst.at[right, low], sems, first + 5, to_left),
-        ]
+    def __init__(self, src, dst, sems, first):
+        me = along_x(0)
+        self.copies = []
+        for i, step in enumerate((2, 1, 3)):
+            device = along_x(step)
+            self.copies.append(
+                remote(src.at[device], dst.at[me], sems, first + i, {"head": device})
+            )
 
     def start(self):
-        for c in self.far + self.near:
-            c.start()
-
-    def relay(self):
-        for c, d in zip(self.far, self.onward):
-            c.wait_recv()
-            d.start()
+        start(self.copies)
 
     def wait(self):
-        for c in self.far:
-            c.wait_send()
-        for c in self.near + self.onward:
-            c.wait()
+        wait(self.copies)
 
 
 class Ring:
@@ -313,6 +295,7 @@
 CHUNKS = 12
 CHUNK = 128
 ROW_CHUNKS = 8
+HALF = 384
 HBM = pl.BlockSpec(memory_space=pltpu.HBM)
 
 
@@ -321,22 +304,35 @@
     return (row < length).astype(F32)[:, 0:1]
 
 
-def add_rows(ref, w_own, grad_up, grad_down, first=False):
-    def step(f, carry):
-        here = pl.ds(pl.multiple_of(f * TILE, TILE), TILE)
+def add_rows(ref, w_own, grad_up, grad_down, first=False, parts=None):
+    if parts:
+        several = [halves(ref.at[part]) for part in parts]
+        sent, grad = (jnp.concatenate(v) for v in zip(*several))
+    else:
         sent, grad = halves(ref)
-        hidden, grad_pre = units(sent, grad, w_own[0, here, :], w_own[1, here, :])
-        one_up = dot(sent, grad_pre, TN)
-        one_down = dot(hidden, grad, TN)
+    tiles = [slice(f, f + TILE) for f in range(0, 768, TILE)]
+
+    def products(here):
+        return dot(sent, w_own[0, here, :], NT), dot(grad, w_own[1, here, :], NT)
+
+    ahead = products(tiles[0])
+    for f, here in enumerate(tiles):
+        pre, grad_hidden = ahead
+        if f + 1 < len(tiles):
+            ahead = products(tiles[f + 1])
+        value, slope = gelu_both(pre)
+        one_up = dot(sent, (grad_hidden * slope).astype(BF), TN)
+        one_down = dot(value.astype(BF), grad, TN)
         if first:
             grad_up[:, here] = one_up
             grad_down[here, :] = one_down
         else:
             grad_up[:, here] += one_up
             grad_down[here, :] += one_down
-        return carry
-
-    lax.fori_loop(0, 768 // TILE, step, 0)
+
+
+def row_chunk(n, k):
+    return pl.ds(k * (n // ROW_CHUNKS), n // ROW_CHUNKS)
 
 
 class Copies:
@@ -376,6 +372,7 @@
     right_rows,
     up_out,
     down_out,
+    got_out,
     tokens,
     cotangent,
     wq_wide,
@@ -388,7 +385,6 @@
     wo_full,
     o,
     o_rows,
-    o_relay,
     lse,
     x_one,
     gates_wide,
@@ -422,8 +418,7 @@
 ):
     me, right, across, left = (along_x(s) for s in range(4))
     to_right, to_left = {"head": right}, {"head": left}
-    core = lax.rem(lax.axis_index("dp"), 2)
-    partner = {"dp": lax.axis_index("dp") + 1 - 2 * core}
+    partner = {"dp": lax.axis_index("dp") + 1 - 2 * lax.rem(lax.axis_index("dp"), 2)}
     rows = tokens.shape[0]
     experts = router.shape[0]
     loads, saves = Copies(local), Copies(saved)
@@ -444,7 +439,37 @@
     for c in range(3):
         w_low[256 * c : 256 * c + 192, :] = wq_wide[c].astype(BF)
     load_out.wait()
-    wo_full[me] = wo_wide[...].astype(BF)
+    wo_full[0] = wo_wide[...].astype(BF)
+
+    dp = lax.axis_index("dp")
+    y, z, core = place_of(dp)
+    chip = dp // 2
+    has_part = chip < 12
+    w_lanes = pl.ds(pl.multiple_of(core * HALF, 128), HALF)
+    w_rows = pl.ds(pl.multiple_of(jnp.minimum(chip, 11) * 16, 16), 16)
+    wo_sems = (wo_send, wo_recv)
+    along = [
+        remote(
+            wo_full.at[0, w_rows, w_lanes],
+            wo_full.at[4 - s, w_rows, w_lanes],
+            wo_sems,
+            s - 1,
+            {"head": along_x(s)},
+        )
+        for s in X_PEERS
+    ]
+    steps = [(dy, dz) for dy, dz, dc in targets() if dc == 0]
+    spread = []
+    for i, (dy, dz) in enumerate(steps):
+        ref = wo_full.at[pl.ds(1, 3), w_rows, w_lanes]
+        spread.append(remote(ref, ref, wo_sems, 3 + i, {"dp": dp_of(y + dy, z + dz, core)}))
+
+    @pl.when(has_part)
+    def _():
+        start(along)
+
+    def from_part(dy, dz):
+        return dp_of(y + 4 - dy, z + 4 - dz, core) // 2 < 12
 
     def project(block):
         result = dot(a_full[block], w_low[...], NT).astype(BF)
@@ -454,9 +479,6 @@
 
     project(me)
     ring.relay()
-    mine = pl.multiple_of(core * 96, 96)
-    wo_ring = Ring(wo_full, (mine, 96), (wo_send, wo_recv), 0)
-    wo_ring.start()
     load_up.wait()
     w_own[0] = up_wide[...].T.astype(BF)
     load_down.wait()
@@ -478,10 +500,16 @@
 
     ring.first[2].wait_recv()
     project(left)
-    wo_ring.relay()
     send_weights(2)
     ring.first[3].wait_recv()
     project(right)
+
+    @pl.when(has_part)
+    def _():
+        for c in along:
+            c.wait_recv()
+        start(spread)
+
     for c in ring.onward:
         c.wait_recv()
     project(across)
@@ -489,35 +517,35 @@
     saves.start(qkv, qkv_out)
     attend(length_ref[0], qkv, o, lse)
     saves.start(lse, lse_out)
-    swap = Swap(o, o_rows, o_relay, (o_send, o_recv), 0)
+    swap = Swap(o, o_rows, (o_send, o_recv), 0)
     swap.start()
-    for c in wo_ring.first[2:4] + wo_ring.onward:
-        c.wait_recv()
-    share = pl.ds(mine, 96)
-    halves_over = []
-    for i, block in enumerate((left, right, across)):
-        ref = wo_full.at[block, share]
-        halves_over.append(remote(ref, ref, (wo_send, wo_recv), 6 + i, partner))
-    start(halves_over)
+    send_weights(2)
+    for c, (dy, dz) in zip(spread, steps):
+
+        @pl.when(from_part(dy, dz))
+        def _(c=c):
+            c.wait_recv()
+
+    ref = wo_full.at[pl.ds(1, 3), pl.ds(0, 192), w_lanes]
+    half_over = remote(ref, ref, wo_sems, 18, partner)
+    half_over.start()
     o_rows[me] = o[me]
-    spread, pick = picks(routes[...], experts, rows)
+    named, pick = picks(routes[...], experts, rows)
     row = lax.broadcasted_iota(jnp.int32, (rows, rows), 0)
     col = lax.broadcasted_iota(jnp.int32, (rows, rows), 1)
     earlier = dot((col < row).astype(BF), pick.astype(BF))
     slot = jnp.sum(earlier * pick, axis=-1, keepdims=True)
-    target = spread[:, 0:1] * CAP + slot
+    target = named[:, 0:1] * CAP + slot
     lane = lax.broadcasted_iota(jnp.int32, (rows, experts * CAP), 1).astype(F32)
     place[...] = (lane == target).astype(BF)
     saves.start(place, place_out)
-    swap.relay()
-    send_weights(2)
-    wait(halves_over)
+    half_over.wait()
     saves.start(wo_full, wo_out)
     swap.wait()
     saves.start(o_rows, o_out)
-    attention = dot(o_rows[0][:, 0:192], wo_full[0])
+    attention = dot(o_rows[me][:, 0:192], wo_full[0])
     for j in range(1, N_HEAD):
-        attention = attention + dot(o_rows[j][:, 0:192], wo_full[j])
+        attention = attention + dot(o_rows[along_x(j)][:, 0:192], wo_full[j])
     x = tokens[...].astype(F32) + attention
     x_one[...] = x
     saves.start(x_one, x_out)
@@ -539,6 +567,7 @@
     send_weights(CHUNKS - 4)
     wait(over)
 
+    saves.start(got, got_out)
     onward = []
 
     def pass_weights(first, last):
@@ -576,10 +605,11 @@
     pass_weights(3, CHUNKS // 2)
     n = got.shape[0]
     round_rows = []
-    for k in range(ROW_CHUNKS):
-        part = pl.ds(k * (n // ROW_CHUNKS), n // ROW_CHUNKS)
+    for k in range(ROW_CHUNKS - 1):
         sems = (r_send, r_recv)
+        part = row_chunk(n, k)
         round_rows.append(remote(got.at[part], left_rows.at[part], sems, 2 * k, to_right))
+        part = row_chunk(n, ROW_CHUNKS - 1 - k)
         round_rows.append(
             remote(got.at[part], right_rows.at[part], sems, 2 * k + 1, to_left)
         )
@@ -605,7 +635,12 @@
     for c in weights + onward:
         c.wait_send()
     ring.wait_send()
-    wo_ring.wait_send()
+
+    @pl.when(has_part)
+    def _():
+        for c in along + spread:
+            c.wait_send()
+
     wait(saves.started)
 
 
@@ -629,6 +664,7 @@
         out(slots, BF),
         out((width, 768), F32),
         out((768, width), F32),
+        out(slots, BF),
     )
     return pl.pallas_call(
         front_kernel,
@@ -648,7 +684,6 @@
             pltpu.VMEM((N_HEAD, 192, width), BF),
             pltpu.VMEM((N_HEAD, rows, 256), BF),
             pltpu.VMEM((N_HEAD, rows, 256), BF),
-            pltpu.VMEM((2, rows // 2, 256), BF),
             pltpu.VMEM((N_HEAD * rows, 128), F32),
             pltpu.VMEM((rows, width), F32),
             pltpu.VMEM((rows, 128), F32),
@@ -658,10 +693,10 @@
             *[pltpu.VMEM((2, 768, width), BF)] * 4,
             *[pltpu.VMEM((experts * CAP, width), F32)] * 2,
             pltpu.SemaphoreType.DMA((8,)),
-            pltpu.SemaphoreType.DMA((12,)),
+            pltpu.SemaphoreType.DMA((13,)),
             *dma(6),
-            *dma(9),
-            *dma(6),
+            *dma(19),
+            *dma(3),
             *dma(N_DP - 1),
             *dma(2 * CHUNKS),
             *dma(CHUNKS),
@@ -717,7 +752,6 @@
             c.wait_send()
 
 
-HALF = 384
 BLOCK = 48
 LATER = 8
 
@@ -744,6 +778,7 @@
     a_in,
     right_in,
     tokens_in,
+    got_in,
     output_out,
     input_out,
     grad_out_w,
@@ -773,7 +808,6 @@
     across_rows,
     to_heads,
     grad_heads,
-    relay,
     keys_sum,
     values_sum,
     grad_qkv,
@@ -801,6 +835,8 @@
     tiles_x,
     whole,
     every,
+    late,
+    late_all,
     o_send,
     o_recv,
     r_send,
@@ -811,37 +847,41 @@
     c_recv,
     y_send,
     y_recv,
+    l_send,
+    l_recv,
     local,
     saved,
 ):
     loads, saves = Copies(local), Copies(saved)
-    first_loads = [
-        loads.start(src, dst)
-        for src, dst in (
-            (returned_in, returned),
-            (place_in, place),
-            (gates_wide_in, gates_in),
-            (x_in, x_one),
-            (cotangent_in, cotangent),
-            (wo_in, wo_full),
-        )
-    ]
-    load_o = loads.start(o_in, o_rows)
-    rows_loads = [
-        loads.start(src, dst)
-        for src, dst in (
-            (left_in, left_rows),
-            (w_own_in, w_own),
-            (up_in, grad_up),
-            (down_in, grad_down),
-        )
-    ]
-    heads_loads = [loads.start(qkv_in, qkv), loads.start(lse_in, lse)]
-    later_loads = [
-        loads.start(src, dst)
-        for src, dst in ((w_low_in, w_low), (a_in, a_full), (right_in, right_rows))
-    ]
-    load_tokens = loads.start(tokens_in, tokens)
+
+    def load(*pairs):
+        return [loads.start(src, dst) for src, dst in pairs]
+
+    first_loads = load(
+        (returned_in, returned),
+        (place_in, place),
+        (gates_wide_in, gates_in),
+        (x_in, x_one),
+        (cotangent_in, cotangent),
+        (wo_in, wo_full),
+    )
+    n = left_in.shape[0]
+    had = n - n // ROW_CHUNKS
+    left_had, right_had = pl.ds(0, had), pl.ds(n - had, had)
+    load_o = load((o_in, o_rows))
+    rows_loads = load(
+        (left_in.at[left_had], left_rows.at[left_had]),
+        (w_own_in, w_own),
+        (up_in, grad_up),
+        (down_in, grad_down),
+    )
+    heads_loads = load((qkv_in, qkv), (lse_in, lse))
+    later_loads = load(
+        (w_low_in, w_low),
+        (a_in, a_full),
+        (right_in.at[right_had], right_rows.at[right_had]),
+        (tokens_in, tokens),
+    )
     me, right, across, left = (along_x(s) for s in range(4))
     to_right, to_left = {"head": right}, {"head": left}
     dp = lax.axis_index("dp")
@@ -852,22 +892,39 @@
     chips = [lax.rem(y + dy, 4) * 4 + lax.rem(z + dz, 4) for dy, dz in steps]
     peers = [{"dp": 2 * t + core} for t in chips]
     others = [{"head": along_x(s)} for s in (2, 1, 3)]
-    greet([partner] + peers + others)
+    near_dp = [
+        {"dp": dp_of(y, z + s, core + c)} for c in (0, 1) for s in (2, 1, 3, 0) if c + s
+    ]
+    far_devices = [
+        {"dp": dp_of(y + s, z, core), "head": along_x(t)}
+        for s, t in [(2, 2), (2, 1), (1, 2), (2, 3), (3, 2), (2, 0), (0, 2), (1, 1)]
+        + [(3, 3), (1, 3), (3, 1), (1, 0), (0, 1), (3, 0), (0, 3)]
+    ]
+    both_ways = [far_devices[i] for i in (0, 1, 2, 3, 4, 7, 8, 9, 10)]
+    greet(peers + near_dp[3:] + both_ways + others)
     rows, width = x_one.shape
     experts = router.shape[0]
-    n = left_in.shape[0]
+    many = len(steps)
+
+    sems = (r_send, r_recv)
+    part = row_chunk(n, ROW_CHUNKS - 1)
+    rest = [remote(got_in.at[part], left_rows.at[part], sems, 0, to_right)]
+    part = row_chunk(n, 0)
+    rest.append(remote(got_in.at[part], right_rows.at[part], sems, 1, to_left))
+    start(rest)
     size = n // (2 * LATER)
     later = []
-    sems = (r_send, r_recv)
     for k in range(LATER):
         top, low = pl.ds(k * size, size), pl.ds(n // 2 + k * size, size)
-        later.append(remote(left_in.at[top], across_rows.at[top], sems, 2 * k, to_right))
         later.append(
-            remote(right_in.at[low], across_rows.at[low], sems, 2 * k + 1, to_left)
+            remote(left_in.at[top], across_rows.at[top], sems, 2 * k + 2, to_right)
+        )
+        later.append(
+            remote(right_in.at[low], across_rows.at[low], sems, 2 * k + 3, to_left)
         )
     start(later[0:4])
+
     wait(first_loads)
-
     to_slots = place[...]
     result, grad_sent = halves(returned)
     combined = dot(to_slots, result)
@@ -884,30 +941,43 @@
     low = grad_x.astype(BF)
     to_heads[:, :, 192:256] = jnp.zeros((N_HEAD, rows, 64), BF)
     for j in range(N_HEAD):
-        to_heads[j, :, 0:192] = dot(low, wo_full[j], NT).astype(BF)
-    swap = Swap(to_heads, grad_heads, relay, (o_send, o_recv), 0)
+        to_heads[along_x(j), :, 0:192] = dot(low, wo_full[j], NT).astype(BF)
+    swap = Swap(to_heads, grad_heads, (o_send, o_recv), 0)
     swap.start()
     grad_heads[me] = to_heads[me]
-    grad_x_one[...] = grad_x
-    output[...] = (x + gates * combined).astype(BF)
-    saves.start(output, output_out)
 
     theirs = pl.ds(pl.multiple_of((1 - core) * HALF, 128), HALF)
     ours = pl.ds(pl.multiple_of(core * HALF, 128), HALF)
-    load_o.wait()
-    for j in range(N_HEAD):
-        out_sum[j] = dot(o_rows[j][:, 0:192], low, TN)
-    swap.relay()
-    start(later[4:])
-    out_cross[...] = out_sum[:, :, theirs].astype(BF)
-    joined = remote(out_cross, out_cross_in, (c_send, c_recv), 0, partner)
-    joined.start()
     small[...] = jnp.zeros_like(small)
     small[2:3, :] = jnp.sum(grad_h * xhat, axis=0, keepdims=True)
     small[3:4, :] = jnp.sum(grad_h, axis=0, keepdims=True)
     h_two = xhat * gain + norms[3:4, :]
     small[8 : 8 + experts, :] = dot(columns, h_two, TN, PRECISE)
-
+    over_small = remote(small.at[:, theirs], small_peer, (c_send, c_recv), 2, partner)
+    over_small.start()
+
+    wait(load_o)
+    for j in range(N_HEAD):
+        out_sum[j] = dot(o_rows[j][:, 0:192], low, TN)
+    out_cross[...] = out_sum[:, :, theirs].astype(BF)
+    joined = remote(out_cross, out_cross_in, (c_send, c_recv), 0, partner)
+    joined.start()
+    grad_x_one[...] = grad_x
+    output[...] = (x + gates * combined).astype(BF)
+    saves.start(output, output_out)
+    over_small.wait_recv()
+    for t in range(15):
+        r, l = 8 * (t // 3), 128 * (t % 3)
+        where = pl.ds(pl.multiple_of(core * HALF + l, 128), 128)
+        tile_mine[t] = small[r : r + 8, where] + small_peer[r : r + 8, l : l + 128]
+    tile_mine[15] = jnp.zeros((8, 128), F32)
+    sems = (y_send, y_recv)
+    base = 0
+    tile_sums = []
+    for i, t in enumerate(chips):
+        tile_sums.append(remote(tile_mine.at[t], tiles.at[i], sems, base + i, peers[i]))
+    start(tile_sums)
+    base += many
     joined.wait_recv()
 
     def out_block(block):
@@ -918,34 +988,44 @@
     )
     out_ring.send_far(out_block(across))
     wait(rows_loads)
+    wait(rest)
     add_rows(left_rows, w_own, grad_up, grad_down)
     swap.wait()
+    for c in tile_sums:
+        c.wait_recv()
+    tile = tile_mine[chip]
+    for i in range(many):
+        tile = tile + tiles[i]
+    tiles_x[me] = tile
+    swaps = []
+    for i, device in enumerate(others):
+        ref = tiles_x.at[me]
+        swaps.append(remote(ref, ref, sems, base + i, device))
+    start(swaps)
+    base += 3
+    start(later[4:12])
+
     wait(heads_loads)
-
     attend_back(length_ref[0], qkv, lse, grad_heads, grad_qkv, keys_sum, values_sum)
-
     wait(later_loads)
 
     def partial(block):
         here = pl.ds(pl.multiple_of(block * rows, rows), rows)
-        total = dot(grad_qkv[0, here, :], w_low[0:256, :])
-        total = total + dot(grad_qkv[1, here, :], w_low[256:512, :])
-        return total + dot(grad_qkv[2, here, :], w_low[512:768, :])
+        joint = jnp.concatenate([grad_qkv[c, here, :] for c in range(3)], axis=1)
+        return dot(joint, w_low[...])
 
     in_ring = RingSum(far, near, from_far, from_near, (h_send, h_recv), 0)
     in_ring.send_far(partial(across))
     out_ring.send_near(out_block(right), out_block(left))
     out_own = out_block(me)
     for c in range(3):
-        total = dot(grad_qkv[c, 0:rows, :], a_full[0], TN)
-        for j in range(1, N_HEAD):
-            here = slice(j * rows, (j + 1) * rows)
-            total = total + dot(grad_qkv[c, here, :], a_full[j], TN)
+        total = dot(grad_qkv[c], a_full[...].reshape(N_HEAD * rows, width), TN)
         out_sum[c] = total[0:192, :]
     cross[...] = out_sum[0:3, :, theirs].astype(BF)
     crossed = remote(cross, cross_in, (c_send, c_recv), 1, partner)
     crossed.start()
     in_ring.send_near(partial(right), partial(left))
+    start(later[12:])
     grad_in = partial(me)
     mine[576:768, :] = out_own + out_ring.arrived()
     crossed.wait_recv()
@@ -953,26 +1033,33 @@
         here = slice(192 * c, 192 * c + 192)
         mine[here, :] = out_sum[c, :, ours] + cross_in[c].astype(F32)
     low_mine[...] = mine[...].astype(BF)
-    sems = (y_send, y_recv)
-    base = 0
-    many = len(steps)
     sums = []
     for i, t in enumerate(chips):
         src = low_mine.at[pl.ds(pl.multiple_of(t * BLOCK, BLOCK), BLOCK)]
         sums.append(remote(src, pieces.at[i], sems, base + i, peers[i]))
     start(sums)
     base += many
+    for c in swaps:
+        c.wait_recv()
+    every[core, chip] = (tiles_x[0] + tiles_x[1]) + (tiles_x[2] + tiles_x[3])
+    spreads = []
+    for i in range(many):
+        ref = every.at[core, chip]
+        spreads.append(remote(ref, ref, sems, base + i, peers[i]))
+    start(spreads)
+    base += many
 
     add_rows(right_rows, w_own, grad_up, grad_down)
-    load_tokens.wait()
     grad_in = grad_in + in_ring.arrived()
     xhat, scale = normed(tokens[...].astype(F32))
     input_grad[...] = grad_x_one[...] + norm_back(grad_in, norms[0:1, :], xhat, scale)
     saves.start(input_grad, input_out)
-    small[0:1, :] = jnp.sum(grad_in * xhat, axis=0, keepdims=True)
-    small[1:2, :] = jnp.sum(grad_in, axis=0, keepdims=True)
-    over_small = remote(small.at[:, theirs], small_peer, (c_send, c_recv), 2, partner)
-    over_small.start()
+    late[...] = jnp.zeros_like(late)
+    gain_grad = jnp.sum(grad_in * xhat, axis=0, keepdims=True)
+    shift_grad = jnp.sum(grad_in, axis=0, keepdims=True)
+    for k in range(6):
+        late[k : k + 1, :] = gain_grad[:, 128 * k : 128 * k + 128]
+        late[k + 6 : k + 7, :] = shift_grad[:, 128 * k : 128 * k + 128]
 
     for c in sums:
         c.wait_recv()
@@ -987,72 +1074,63 @@
         gathers.append(remote(ref, ref, sems, base + i, peers[i]))
     start(gathers)
     base += many
-    over_small.wait_recv()
-    for t in range(15):
-        r, l = 8 * (t // 3), 128 * (t % 3)
-        where = pl.ds(pl.multiple_of(core * HALF + l, 128), 128)
-        tile_mine[t] = small[r : r + 8, where] + small_peer[r : r + 8, l : l + 128]
-    tile_mine[15] = jnp.zeros((8, 128), F32)
-    tile_sums = []
-    for i, t in enumerate(chips):
-        tile_sums.append(remote(tile_mine.at[t], tiles.at[i], sems, base + i, peers[i]))
-    start(tile_sums)
-    base += many
-    wait(later)
-    add_rows(across_rows, w_own, grad_up, grad_down)
+    for c in spreads:
+        c.wait_recv()
+    last_small = remote(every.at[core], every.at[core], sems, base, partner)
+    last_small.start()
+    base += 1
+    for first, last in ((0, LATER // 2), (LATER // 2, LATER)):
+        wait(later[2 * first : 2 * last])
+        count = (last - first) * size
+        parts = [pl.ds(first * size, count), pl.ds(n // 2 + first * size, count)]
+        add_rows(across_rows, w_own, grad_up, grad_down, parts=parts)
     saves.start(grad_up, up_out)
     saves.start(grad_down, down_out)
     squares = sum_squares(grad_up[...]) + sum_squares(grad_down[...]) + sum_squares(piece)
-    for c in tile_sums:
-        c.wait_recv()
-    tile = tile_mine[chip]
-    for i in range(many):
-        tile = tile + tiles[i]
-    tiles_x[me, 0] = tile
-    tiles_x[me, 1] = jnp.broadcast_to(squares, (8, 128))
-    swaps = []
-    for i, device in enumerate(others):
-        ref = tiles_x.at[me]
-        swaps.append(remote(ref, ref, sems, base + i, device))
-    start(swaps)
-    base += 3
+    late[12:13, :] = jnp.broadcast_to(squares, (1, 128))
+
+    late_copies = []
+
+    def over(level, place, many, devices):
+        late_all[level, place] = late[...]
+        ref = late_all.at[level, place]
+        copies = []
+        for device in devices:
+            i = len(late_copies)
+            copies.append(remote(ref, ref, (l_send, l_recv), i, device))
+            late_copies.append(copies[-1])
+        start(copies)
+        for c in copies:
+            c.wait_recv()
+        total = late_all[level, 0] + late_all[level, 1]
+        for k in range(2, many, 2):
+            total = total + (late_all[level, k] + late_all[level, k + 1])
+        late[...] = total
+
+    over(0, 2 * z + core, 8, near_dp)
+    over(1, 4 * y + me, 16, far_devices)
+
+    last_small.wait_recv()
+    for c in range(2):
+        for t in range(15):
+            r, l = 8 * (t // 3), 128 * (t % 3)
+            small_out[r : r + 8, HALF * c + l : HALF * c + l + 128] = every[c, t]
+    for k in range(6):
+        lanes = slice(128 * k, 128 * k + 128)
+        small_out[0:1, lanes] = late[k : k + 1, :]
+        small_out[1:2, lanes] = late[k + 6 : k + 7, :]
+    total = late[12:13, 0:1] + sum_squares(small_out[...])
+    norm_out[...] = jnp.broadcast_to(jnp.sqrt(total), norm_out.shape)
     for c in gathers:
         c.wait_recv()
     last = remote(whole.at[core], whole.at[core], sems, base, partner)
     last.start()
-    base += 1
-    for c in swaps:
-        c.wait_recv()
-    tile = (tiles_x[0, 0] + tiles_x[1, 0]) + (tiles_x[2, 0] + tiles_x[3, 0])
-    score = (tiles_x[0, 1] + tiles_x[1, 1]) + (tiles_x[2, 1] + tiles_x[3, 1])
-    every[core, chip, 0] = tile
-    every[core, chip, 1] = score + jnp.broadcast_to(sum_squares(tile), (8, 128))
-    spreads = []
-    for i in range(many):
-        ref = every.at[core, chip]
-        spreads.append(remote(ref, ref, sems, base + i, peers[i]))
-    start(spreads)
-    base += many
     last.wait_recv()
     grad_out_w[:, 0:HALF] = whole[0]
     grad_out_w[:, HALF : 2 * HALF] = whole[1]
-    for c in spreads:
-        c.wait_recv()
-    last_small = remote(every.at[core], every.at[core], sems, base, partner)
-    last_small.start()
-    last_small.wait_recv()
-    total = every[0, 0, 1]
-    for c in range(2):
-        for t in range(N_CHIP):
-            if c + t:
-                total = total + every[c, t, 1]
-            if t < 15:
-                r, l = 8 * (t // 3), 128 * (t % 3)
-                small_out[r : r + 8, HALF * c + l : HALF * c + l + 128] = every[c, t, 0]
-    norm_out[...] = jnp.sqrt(total)
     out_ring.wait_send()
     in_ring.wait_send()
-    for c in [joined, crossed, over_small, last, last_small]:
+    for c in [joined, crossed, over_small, last, last_small] + late_copies:
         c.wait_send()
     for c in sums + gathers + tile_sums + swaps + spreads:
         c.wait_send()
@@ -1075,7 +1153,7 @@
             out((width, 768), F32),
             out((768, width), F32),
         ),
-        in_specs=[SM, VM, VM, VM] + [HBM] * 17,
+        in_specs=[SM, VM, VM, VM] + [HBM] * 18,
         out_specs=(HBM, HBM, VM, VM, VM, HBM, HBM),
         scratch_shapes=[
             pltpu.VMEM((rows, width), BF),
@@ -1087,7 +1165,6 @@
             pltpu.VMEM(slots, BF),
             pltpu.VMEM((N_HEAD, rows, 256), BF),
             pltpu.VMEM((N_HEAD, rows, 256), BF),
-            pltpu.VMEM((2, rows // 2, 256), BF),
             pltpu.VMEM((qkv[1], 256), F32),
             pltpu.VMEM((qkv[1], 256), F32),
             pltpu.VMEM(qkv, BF),
@@ -1112,14 +1189,17 @@
             pltpu.VMEM((40, HALF), F32),
             pltpu.VMEM((N_CHIP, 8, 128), F32),
             pltpu.VMEM((many, 8, 128), F32),
-            pltpu.VMEM((N_HEAD, 2, 8, 128), F32),
+            pltpu.VMEM((N_HEAD, 8, 128), F32),
             pltpu.VMEM((2, 768, HALF), BF),
-            pltpu.VMEM((2, N_CHIP, 2, 8, 128), F32),
-            *dma(6),
-            *dma(2 * LATER),
-            *dma(8),
+            pltpu.VMEM((2, N_CHIP, 8, 128), F32),
+            pltpu.VMEM((16, 128), F32),
+            pltpu.VMEM((2, 16, 16, 128), F32),
+            *dma(3),
+            *dma(2 * LATER + 2),
+            *dma(12),
             *dma(3),
             *dma(4 * many + 5),
+            *dma(22),
             pltpu.SemaphoreType.DMA((18,)),
             pltpu.SemaphoreType.DMA((4,)),
         ],
@@ -1132,76 +1212,88 @@
 def adam_step(gradient, moment_one, moment_two, weight, step_rate):
     first_new = BETA_ONE * moment_one + (1.0 - BETA_ONE) * gradient
     second_new = BETA_TWO * moment_two + (1.0 - BETA_TWO) * gradient * gradient
-    first_hat = first_new / (1.0 - BETA_ONE**STEP)
-    second_hat = second_new / (1.0 - BETA_TWO**STEP)
+    first_hat = first_new * (1.0 / (1.0 - BETA_ONE**STEP))
+    second_hat = second_new * (1.0 / (1.0 - BETA_TWO**STEP))
     weight_new = weight - step_rate * (
         first_hat / (jnp.sqrt(second_hat) + ADAM_EPS) + WEIGHT_DECAY * weight
     )
     return (first_new, second_new, weight_new)
 
 
-RATES = (0.1, 0.5, 0.08, 0.1, 1.0, 0.05)
-ADAM_STEPS = 6
-
-
-def adam_kernel(norm, attn, small, output, input_grad, up, down, *refs):
+RATES = (0.08, 0.1, 0.1, 0.5, 1.0, 0.05)
+PIECES = 2
+
+
+def adam_kernel(norm, attn, small, up_in, down_in, output, input_grad, *refs):
+    moments, results, norm_out = refs[0:18], refs[18:38], refs[38]
+    held, up, down, output_held, input_held, sems, out_sems = refs[39:51], *refs[51:]
+    loads, saves = Copies(sems), Copies(out_sems)
+    waits = {}
+    grads_in = {0: (up_in, up), 1: (down_in, down)}
+    for i in range(4):
+        for p in range(PIECES):
+            n = held[3 * i].shape[0] // PIECES
+            part = pl.ds(p * n, n)
+            pairs = [(moments[3 * i + k], held[3 * i + k]) for k in range(3)]
+            if i in grads_in:
+                pairs.append(grads_in[i])
+            waits[i, p] = [loads.start(src.at[part], dst.at[part]) for src, dst in pairs]
+    passing = [loads.start(output, output_held), loads.start(input_grad, input_held)]
+    norm_out[0] = jnp.max(norm[...])
     factor = jnp.minimum(1.0, CLIP_NORM / (norm[0:1, 0:1] + 1e-06))
-    moments, results, norm_out = refs[0:18], refs[18:38], refs[38]
-    results[18][...] = output[...]
-    results[19][...] = input_grad[...]
-    norm_out[0] = jnp.max(norm[...])
-    step = pl.program_id(0)
-    first, second = up.shape[0] * 3 // 4, up.shape[0] // 4
-    grads = (
-        attn[pl.ds(pl.multiple_of(step * first, 32), first), :],
-        attn[pl.ds(pl.multiple_of(576 + step * second, 32), second), :],
-        up[...],
-        down[...],
-        small[0:4, :],
-        small[8:40, :],
-    )
-
-    def update(i):
+    for i, grad in ((4, small[0:4, :]), (5, small[8:40, :])):
         one, two, weight = (r[...] for r in moments[3 * i : 3 * i + 3])
-        new = adam_step(grads[i].astype(F32) * factor, one, two, weight, RATES[i])
+        new = adam_step(grad * factor, one, two, weight, RATES[i])
         for ref, value in zip(results[3 * i : 3 * i + 3], new):
             ref[...] = value
-
+    wait(passing)
+    saves.start(output_held, results[18])
+    saves.start(input_held, results[19])
+    first = {2: 0, 3: 576}
     for i in range(4):
-        update(i)
-
-    @pl.when(step == 0)
-    def _():
-        update(4)
-        update(5)
-
-
-def adam(norm, attn, small, output, input_grad, up, down, moments):
-    def whole(v):
-        return pl.BlockSpec(v.shape, lambda i: (0, 0))
-
-    def tiled(v):
-        return pl.BlockSpec((v.shape[0] // ADAM_STEPS, v.shape[1]), lambda i: (i, 0))
-
-    def quarter(v):
-        return pl.BlockSpec((v.shape[0] // 4, v.shape[1]), lambda i: (jnp.minimum(i, 3), 0))
-
-    specs = [tiled(v) for v in moments[0:12]] + [whole(v) for v in moments[12:18]]
-    rows = [quarter(output), quarter(input_grad)]
+        for p in range(PIECES):
+            n = held[3 * i].shape[0] // PIECES
+            wait(waits[i, p])
+
+            def step(t, carry, i=i, p=p, n=n):
+                here = pl.ds(pl.multiple_of(p * n + t * 32, 32), 32)
+                if i in grads_in:
+                    grad = grads_in[i][1][here, :]
+                else:
+                    there = pl.ds(pl.multiple_of(first[i] + p * n + t * 32, 32), 32)
+                    grad = attn[there, :].astype(F32)
+                one, two, weight = (held[3 * i + k][here, :] for k in range(3))
+                new = adam_step(grad * factor, one, two, weight, RATES[i])
+                for k in range(3):
+                    held[3 * i + k][here, :] = new[k]
+                return carry
+
+            lax.fori_loop(0, n // 32, step, 0)
+            part = pl.ds(p * n, n)
+            for k in range(3):
+                saves.start(held[3 * i + k].at[part], results[3 * i + k].at[part])
+    wait(saves.started)
+
+
+def adam(norm, attn, small, up, down, output, input_grad, moments):
+    large = moments[0:12]
     return pl.pallas_call(
         adam_kernel,
-        grid=(ADAM_STEPS,),
         out_shape=[out(v.shape, v.dtype) for v in (*moments, output, input_grad)]
         + [out((1,), F32)],
-        in_specs=[whole(norm), whole(attn), whole(small)]
-        + rows
-        + [tiled(up), tiled(down)]
-        + specs,
-        out_specs=specs + rows + [SM],
+        in_specs=[VM] * 3 + [HBM] * 16 + [VM] * 6,
+        out_specs=[HBM] * 12 + [VM] * 6 + [HBM] * 2 + [SM],
+        scratch_shapes=[
+            pltpu.VMEM(v.shape, v.dtype) for v in (*large, up, down, output, input_grad)
+        ]
+        + [
+            pltpu.SemaphoreType.DMA((14 * PIECES + 2,)),
+            pltpu.SemaphoreType.DMA((12 * PIECES + 2,)),
+        ],
         compiler_params=params(None, 58),
         cost_estimate=cost(13),
         name="adamw",
-    )(norm, attn, small, output, input_grad, up, down, *moments)
+    )(norm, attn, small, up, down, output, input_grad, *moments)
 
 
 def swapped(v):
@@ -1250,6 +1342,7 @@
         right_rows,
         part_up,
         part_down,
+        got,
     ) = front(
         lengths,
         norms,
@@ -1284,26 +1377,26 @@
         a_full,
         right_rows,
         tokens,
+        got,
     )
 
     def flat(v):
         return swapped(v).reshape(576, -1)
 
-    moments = [flat(v) for v in (first_qkv, second_qkv, w_qkv)]
-    moments += [first_out, second_out, w_out]
-    moments += [v[0] for v in (first_up, second_up, w_up, first_down, second_down, w_down)]
-    moments += [first_norms, second_norms, norms]
+    moments = [v[0] for v in (first_up, second_up, w_up, first_down, second_down, w_down)]
+    moments += [flat(v) for v in (first_qkv, second_qkv, w_qkv)]
+    moments += [first_out, second_out, w_out, first_norms, second_norms, norms]
     moments += [swapped(v) for v in (first_router, second_router, router)]
-    new = adam(norm, grad_attn, small, output, input_grad, grad_up, grad_down, moments)
+    new = adam(norm, grad_attn, small, grad_up, grad_down, output, input_grad, moments)
     return (
         new[18],
         new[19],
         new[20].reshape(()),
         *new[12:15],
-        *(swapped(v.reshape(3, 192, -1)) for v in new[0:3]),
-        *new[3:6],
+        *(swapped(v.reshape(3, 192, -1)) for v in new[6:9]),
+        *new[9:12],
         *(swapped(v) for v in new[15:18]),
-        *(v[None] for v in new[6:12]),
+        *(v[None] for v in new[0:6]),
     )
 
 

time: 245 us -> 245 us (level); the launches traced: 245 us -> 241 us
  Pallas kernels: 244 us -> 239 us
    pallas_call x1, Pallas kernels: 148 us -> 141 us  [front(): pl.pallas_call(front_kernel, out_shape=outs, in_specs=[SM, VM, VM, VM] +...]
    pallas_call x1, Pallas kernels: 72.7 us -> 78.1 us  [back(): pl.pallas_call(back_kernel, out_shape=(out((rows, width), BF), out((rows,...]
where the time goes in v1:
time: 245 us; the launch traced here: 241 us
  Pallas kernels  239 us (98%)
    pallas_call x1, Pallas kernels, front(): pl.pallas_call(front_kernel, out_shape=outs, in_specs=[SM, VM, VM, VM] +...  141 us
    pallas_call x1, Pallas kernels, back(): pl.pallas_call(back_kernel, out_shape=(out((rows, width), BF), out((rows,...  78.1 us
    pallas_call x1, Pallas kernels, adam(): pl.pallas_call(adam_kernel, out_shape=[out(v.shape, v.dtype) for v in (*m...  20.5 us

profile of v1, /device:TPU:1, one launch (start us, length us, event | category | flops | bytes accessed | tf_op | source)
XLA Modules:
  0.0 240.7 jit_solution(9968718949043051589)
XLA Ops:
  1.3 140.6 %front.1 = (bf16[4,256,768]{2,1,0:T(8,128)(2,1)}, bf16[3,1024,256]{2,1,0:T(8,128)(2,1)}, bf16[768,768]{1,0:T(8,128)(2,1)}, bf16[4,192,768]{2,1,0:T(8,128)(2,1)},...) custom-call(s32[1]{0:T(128)S(6)} %copy.43.length_ref, ...), custom_call_target="tpu_custom_call" | custom-call | flops 142999994368 | bytes 130000000 | tf_op jit(solution)/shard_map/front/pallas_call | solution.py:669
  141.9 78.1 %back.1 = (bf16[256,768]{1,0:T(8,128)(2,1)}, f32[256,768]{1,0:T(8,128)}, bf16[768,768]{1,0:T(8,128)(2,1)}, f32[40,768]{1,0:T(8,128)}, f32[8,128]{1,0:T(8,128)}, /*index=5*/f32[768,768]{1,0:T(8,128)}, f32[768,768]{1,0:T(8,128)}) custom-call(s32[1]{0:T(128)S(6)} %copy.43.length_ref, f32[4,768]{1,0:T(4,128)} %refs_14_.1, f32[32,768]{1,0:T(8,128)} %bitcast.51, ...), custom_call_target="tpu_custom_call" | custom-call | flops 65999998976 | bytes 60000000 | tf_op jit(solution)/shard_map/back/pallas_call | solution.py:1145
  220.0 20.5 %adamw.1 = (f32[768,768]{1,0:T(8,128)}, f32[768,768]{1,0:T(8,128)}, f32[768,768]{1,0:T(8,128)}, f32[768,768]{1,0:T(8,128)}, f32[768,768]{1,0:T(8,128)}, /*index=...) custom-call(f32[8,128]{1,0:T(8,128)} %get-tuple-element.81.norm, ...), custom_call_target="tpu_custom_call" | custom-call | flops 14300000256 | bytes 13000000 | tf_op jit(solution)/shard_map/adamw/pallas_call | solution.py:1280

commit v2 on v1

--- a/solution.py
+++ b/solution.py
@@ -781,7 +781,7 @@
     got_in,
     output_out,
     input_out,
-    grad_out_w,
+    attn_out,
     small_out,
     norm_out,
     up_out,
@@ -1091,7 +1091,7 @@
 
     late_copies = []
 
-    def over(level, place, many, devices):
+    def over(level, place, many, devices, meanwhile):
         late_all[level, place] = late[...]
         ref = late_all.at[level, place]
         copies = []
@@ -1100,6 +1100,7 @@
             copies.append(remote(ref, ref, (l_send, l_recv), i, device))
             late_copies.append(copies[-1])
         start(copies)
+        meanwhile()
         for c in copies:
             c.wait_recv()
         total = late_all[level, 0] + late_all[level, 1]
@@ -1107,27 +1108,30 @@
             total = total + (late_all[level, k] + late_all[level, k + 1])
         late[...] = total
 
-    over(0, 2 * z + core, 8, near_dp)
-    over(1, 4 * y + me, 16, far_devices)
-
-    last_small.wait_recv()
-    for c in range(2):
-        for t in range(15):
-            r, l = 8 * (t // 3), 128 * (t % 3)
-            small_out[r : r + 8, HALF * c + l : HALF * c + l + 128] = every[c, t]
+    last = remote(whole.at[core], whole.at[core], sems, base, partner)
+
+    def send_half():
+        for c in gathers:
+            c.wait_recv()
+        last.start()
+
+    def finish_halves():
+        last_small.wait_recv()
+        for c in range(2):
+            for t in range(15):
+                r, l = 8 * (t // 3), 128 * (t % 3)
+                small_out[r : r + 8, HALF * c + l : HALF * c + l + 128] = every[c, t]
+        last.wait_recv()
+        saves.start(whole, attn_out)
+
+    over(0, 2 * z + core, 8, near_dp, send_half)
+    over(1, 4 * y + me, 16, far_devices, finish_halves)
     for k in range(6):
         lanes = slice(128 * k, 128 * k + 128)
         small_out[0:1, lanes] = late[k : k + 1, :]
         small_out[1:2, lanes] = late[k + 6 : k + 7, :]
     total = late[12:13, 0:1] + sum_squares(small_out[...])
     norm_out[...] = jnp.broadcast_to(jnp.sqrt(total), norm_out.shape)
-    for c in gathers:
-        c.wait_recv()
-    last = remote(whole.at[core], whole.at[core], sems, base, partner)
-    last.start()
-    last.wait_recv()
-    grad_out_w[:, 0:HALF] = whole[0]
-    grad_out_w[:, HALF : 2 * HALF] = whole[1]
     out_ring.wait_send()
     in_ring.wait_send()
     for c in [joined, crossed, over_small, last, last_small] + late_copies:
@@ -1147,14 +1151,14 @@
         out_shape=(
             out((rows, width), BF),
             out((rows, width), F32),
-            out((768, width), BF),
+            out((2, 768, HALF), BF),
             out((40, width), F32),
             out((8, 128), F32),
             out((width, 768), F32),
             out((768, width), F32),
         ),
         in_specs=[SM, VM, VM, VM] + [HBM] * 18,
-        out_specs=(HBM, HBM, VM, VM, VM, HBM, HBM),
+        out_specs=(HBM, HBM, HBM, VM, VM, HBM, HBM),
         scratch_shapes=[
             pltpu.VMEM((rows, width), BF),
             pltpu.VMEM((rows, width), F32),
@@ -1201,7 +1205,7 @@
             *dma(4 * many + 5),
             *dma(22),
             pltpu.SemaphoreType.DMA((18,)),
-            pltpu.SemaphoreType.DMA((4,)),
+            pltpu.SemaphoreType.DMA((5,)),
         ],
         compiler_params=params(3, 58),
         cost_estimate=cost(60),
@@ -1224,9 +1228,9 @@
 PIECES = 2
 
 
-def adam_kernel(norm, attn, small, up_in, down_in, output, input_grad, *refs):
+def adam_kernel(norm, small, attn_in, up_in, down_in, output, input_grad, *refs):
     moments, results, norm_out = refs[0:18], refs[18:38], refs[38]
-    held, up, down, output_held, input_held, sems, out_sems = refs[39:51], *refs[51:]
+    held, up, down, output_held, input_held, attn, sems, out_sems = refs[39:51], *refs[51:]
     loads, saves = Copies(sems), Copies(out_sems)
     waits = {}
     grads_in = {0: (up_in, up), 1: (down_in, down)}
@@ -1238,6 +1242,7 @@
             if i in grads_in:
                 pairs.append(grads_in[i])
             waits[i, p] = [loads.start(src.at[part], dst.at[part]) for src, dst in pairs]
+    load_attn = loads.start(attn_in, attn)
     passing = [loads.start(output, output_held), loads.start(input_grad, input_held)]
     norm_out[0] = jnp.max(norm[...])
     factor = jnp.minimum(1.0, CLIP_NORM / (norm[0:1, 0:1] + 1e-06))
@@ -1251,6 +1256,8 @@
     saves.start(input_held, results[19])
     first = {2: 0, 3: 576}
     for i in range(4):
+        if i == 2:
+            load_attn.wait()
         for p in range(PIECES):
             n = held[3 * i].shape[0] // PIECES
             wait(waits[i, p])
@@ -1261,7 +1268,8 @@
                     grad = grads_in[i][1][here, :]
                 else:
                     there = pl.ds(pl.multiple_of(first[i] + p * n + t * 32, 32), 32)
-                    grad = attn[there, :].astype(F32)
+                    grad = jnp.concatenate([attn[0, there, :], attn[1, there, :]], axis=1)
+                    grad = grad.astype(F32)
                 one, two, weight = (held[3 * i + k][here, :] for k in range(3))
                 new = adam_step(grad * factor, one, two, weight, RATES[i])
                 for k in range(3):
@@ -1275,25 +1283,26 @@
     wait(saves.started)
 
 
-def adam(norm, attn, small, up, down, output, input_grad, moments):
+def adam(norm, small, attn, up, down, output, input_grad, moments):
     large = moments[0:12]
     return pl.pallas_call(
         adam_kernel,
         out_shape=[out(v.shape, v.dtype) for v in (*moments, output, input_grad)]
         + [out((1,), F32)],
-        in_specs=[VM] * 3 + [HBM] * 16 + [VM] * 6,
+        in_specs=[VM] * 2 + [HBM] * 17 + [VM] * 6,
         out_specs=[HBM] * 12 + [VM] * 6 + [HBM] * 2 + [SM],
         scratch_shapes=[
-            pltpu.VMEM(v.shape, v.dtype) for v in (*large, up, down, output, input_grad)
+            pltpu.VMEM(v.shape, v.dtype)
+            for v in (*large, up, down, output, input_grad, attn)
         ]
         + [
-            pltpu.SemaphoreType.DMA((14 * PIECES + 2,)),
+            pltpu.SemaphoreType.DMA((14 * PIECES + 3,)),
             pltpu.SemaphoreType.DMA((12 * PIECES + 2,)),
         ],
         compiler_params=params(None, 58),
         cost_estimate=cost(13),
         name="adamw",
-    )(norm, attn, small, up, down, output, input_grad, *moments)
+    )(norm, small, attn, up, down, output, input_grad, *moments)
 
 
 def swapped(v):
@@ -1387,7 +1396,7 @@
     moments += [flat(v) for v in (first_qkv, second_qkv, w_qkv)]
     moments += [first_out, second_out, w_out, first_norms, second_norms, norms]
     moments += [swapped(v) for v in (first_router, second_router, router)]
-    new = adam(norm, grad_attn, small, grad_up, grad_down, output, input_grad, moments)
+    new = adam(norm, small, grad_attn, grad_up, grad_down, output, input_grad, moments)
     return (
         new[18],
         new[19],

time: 245 us -> 242 us (0.988)
  Pallas kernels: 239 us -> 236 us
    pallas_call x1, Pallas kernels: 78.1 us -> 74.9 us  [back(): pl.pallas_call(back_kernel, out_shape=(out((rows, width), BF), out((rows,...]
where the time goes in v2:
time: 242 us; the launch traced here: 238 us
  Pallas kernels  236 us (98%)
    pallas_call x1, Pallas kernels, front(): pl.pallas_call(front_kernel, out_shape=outs, in_specs=[SM, VM, VM, VM] +...  141 us
    pallas_call x1, Pallas kernels, back(): pl.pallas_call(back_kernel, out_shape=(out((rows, width), BF), out((rows,...  74.9 us
    pallas_call x1, Pallas kernels, adam(): pl.pallas_call(adam_kernel, out_shape=[out(v.shape, v.dtype) for v in (*m...  20.6 us

profile of v2, /device:TPU:1, one launch (start us, length us, event | category | flops | bytes accessed | tf_op | source)
XLA Modules:
  0.0 237.7 jit_solution(2473683157969191618)
XLA Ops:
  1.3 140.6 %front.1 = (bf16[4,256,768]{2,1,0:T(8,128)(2,1)}, bf16[3,1024,256]{2,1,0:T(8,128)(2,1)}, bf16[768,768]{1,0:T(8,128)(2,1)}, bf16[4,192,768]{2,1,0:T(8,128)(2,1)},...) custom-call(s32[1]{0:T(128)S(6)} %copy.43.length_ref, ...), custom_call_target="tpu_custom_call" | custom-call | flops 142999994368 | bytes 130000000 | tf_op jit(solution)/shard_map/front/pallas_call | solution.py:669
  141.9 74.9 %back.1 = (bf16[256,768]{1,0:T(8,128)(2,1)}, f32[256,768]{1,0:T(8,128)}, bf16[2,768,384]{2,1,0:T(8,128)(2,1)}, f32[40,768]{1,0:T(8,128)}, f32[8,128]{1,0:T(8,128...) custom-call(s32[1]{0:T(128)S(6)} %copy.43.length_ref, f32[4,768]{1,0:T(4,128)} %refs_14_.1, f32[32,768]{1,0:T(8,128)} %bitcast.51, ...), custom_call_target="tpu_custom_call" | custom-call | flops 65999998976 | bytes 60000000 | tf_op jit(solution)/shard_map/back/pallas_call | solution.py:1149
  216.8 20.6 %adamw.1 = (f32[768,768]{1,0:T(8,128)}, f32[768,768]{1,0:T(8,128)}, f32[768,768]{1,0:T(8,128)}, f32[768,768]{1,0:T(8,128)}, f32[768,768]{1,0:T(8,128)}, /*index=...) custom-call(f32[8,128]{1,0:T(8,128)} %get-tuple-element.81.norm, ...), custom_call_target="tpu_custom_call" | custom-call | flops 14300000256 | bytes 13000000 | tf_op jit(solution)/shard_map/adamw/pallas_call | solution.py:1288

commit v3 on v2

--- a/solution.py
+++ b/solution.py
@@ -162,6 +162,11 @@
     lax.fori_loop(0, 3, one_head, 0)
     grad_qkv[1] = keys_sum[...].astype(BF)
     grad_qkv[2] = values_sum[...].astype(BF)
+
+
+def spread_out(rows):
+    nothing = jnp.zeros_like(rows)
+    return jnp.concatenate([rows, nothing]), jnp.concatenate([nothing, rows])
 
 
 class Swap:
@@ -384,6 +389,7 @@
     w_low,
     wo_full,
     o,
+    o_packed,
     o_rows,
     lse,
     x_one,
@@ -517,7 +523,13 @@
     saves.start(qkv, qkv_out)
     attend(length_ref[0], qkv, o, lse)
     saves.start(lse, lse_out)
-    swap = Swap(o, o_rows, (o_send, o_recv), 0)
+    half = rows // 2
+    for i in range(N_HEAD):
+        o_packed[i, 0:rows, :] = o[i, :, 0:128]
+        third = o[i, :, 128:256].astype(F32)
+        both = third[0:half, :] + pltpu.roll(third[half:, :], 64, 1)
+        o_packed[i, rows:, :] = both.astype(BF)
+    swap = Swap(o_packed, o_rows, (o_send, o_recv), 0)
     swap.start()
     send_weights(2)
     for c, (dy, dz) in zip(spread, steps):
@@ -529,7 +541,7 @@
     ref = wo_full.at[pl.ds(1, 3), pl.ds(0, 192), w_lanes]
     half_over = remote(ref, ref, wo_sems, 18, partner)
     half_over.start()
-    o_rows[me] = o[me]
+    o_rows[me] = o_packed[me]
     named, pick = picks(routes[...], experts, rows)
     row = lax.broadcasted_iota(jnp.int32, (rows, rows), 0)
     col = lax.broadcasted_iota(jnp.int32, (rows, rows), 1)
@@ -543,9 +555,12 @@
     saves.start(wo_full, wo_out)
     swap.wait()
     saves.start(o_rows, o_out)
-    attention = dot(o_rows[me][:, 0:192], wo_full[0])
-    for j in range(1, N_HEAD):
-        attention = attention + dot(o_rows[along_x(j)][:, 0:192], wo_full[j])
+    attention = jnp.zeros((rows, tokens.shape[1]), F32)
+    for j in range(N_HEAD):
+        heads = o_rows[along_x(j)]
+        to_top, to_low = spread_out(wo_full[j, 128:192, :])
+        third = [dot(heads[rows:, :], w) for w in (to_top, to_low)]
+        attention = attention + (dot(heads[0:rows, :], wo_full[j, 0:128, :]) + jnp.concatenate(third))
     x = tokens[...].astype(F32) + attention
     x_one[...] = x
     saves.start(x_one, x_out)
@@ -653,7 +668,7 @@
         out((3, N_HEAD * rows, 256), BF),
         out((768, width), BF),
         out((N_HEAD, 192, width), BF),
-        out((N_HEAD, rows, 256), BF),
+        out((N_HEAD, rows + rows // 2, 128), BF),
         out((N_HEAD * rows, 128), F32),
         out((rows, width), F32),
         out((rows, 128), F32),
@@ -683,7 +698,8 @@
             pltpu.VMEM((768, width), BF),
             pltpu.VMEM((N_HEAD, 192, width), BF),
             pltpu.VMEM((N_HEAD, rows, 256), BF),
-            pltpu.VMEM((N_HEAD, rows, 256), BF),
+            pltpu.VMEM((N_HEAD, rows + rows // 2, 128), BF),
+            pltpu.VMEM((N_HEAD, rows + rows // 2, 128), BF),
             pltpu.VMEM((N_HEAD * rows, 128), F32),
             pltpu.VMEM((rows, width), F32),
             pltpu.VMEM((rows, 128), F32),
@@ -807,6 +823,7 @@
     tokens,
     across_rows,
     to_heads,
+    heads_packed,
     grad_heads,
     keys_sum,
     values_sum,
@@ -939,12 +956,15 @@
     gain = norms[2:3, :]
     grad_x = grad_out + norm_back(grad_h, gain, xhat, scale)
     low = grad_x.astype(BF)
-    to_heads[:, :, 192:256] = jnp.zeros((N_HEAD, rows, 64), BF)
+    half = rows // 2
     for j in range(N_HEAD):
-        to_heads[along_x(j), :, 0:192] = dot(low, wo_full[j], NT).astype(BF)
-    swap = Swap(to_heads, grad_heads, (o_send, o_recv), 0)
+        to_heads[along_x(j), 0:rows, :] = dot(low, wo_full[j, 0:128, :], NT).astype(BF)
+        to_top, to_low = spread_out(wo_full[j, 128:192, :])
+        third = dot(low[0:half, :], to_top, NT) + dot(low[half:, :], to_low, NT)
+        to_heads[along_x(j), rows:, :] = third.astype(BF)
+    swap = Swap(to_heads, heads_packed, (o_send, o_recv), 0)
     swap.start()
-    grad_heads[me] = to_heads[me]
+    heads_packed[me] = to_heads[me]
 
     theirs = pl.ds(pl.multiple_of((1 - core) * HALF, 128), HALF)
     ours = pl.ds(pl.multiple_of(core * HALF, 128), HALF)
@@ -958,7 +978,10 @@
 
     wait(load_o)
     for j in range(N_HEAD):
-        out_sum[j] = dot(o_rows[j][:, 0:192], low, TN)
+        out_sum[j, 0:128, :] = dot(o_rows[j, 0:rows, :], low, TN)
+        third = o_rows[j, rows:, :]
+        out_sum[j, 128:192, :] = dot(third, low[0:half, :], TN)[0:64, :]
+        out_sum[j, 128:192, :] += dot(third, low[half:, :], TN)[64:128, :]
     out_cross[...] = out_sum[:, :, theirs].astype(BF)
     joined = remote(out_cross, out_cross_in, (c_send, c_recv), 0, partner)
     joined.start()
@@ -1006,6 +1029,11 @@
     start(later[4:12])
 
     wait(heads_loads)
+    for i in range(N_HEAD):
+        grad_heads[i, :, 0:128] = heads_packed[i, 0:rows, :]
+        third = heads_packed[i, rows:, :]
+        grad_heads[i, 0:half, 128:256] = third
+        grad_heads[i, half:, 128:256] = pltpu.roll(third.astype(F32), 64, 1).astype(BF)
     attend_back(length_ref[0], qkv, lse, grad_heads, grad_qkv, keys_sum, values_sum)
     wait(later_loads)
 
@@ -1167,7 +1195,8 @@
             *[pltpu.VMEM(v.shape, v.dtype) for v in args[4:13]],
             *[pltpu.VMEM(v.shape, v.dtype) for v in args[15:21]],
             pltpu.VMEM(slots, BF),
-            pltpu.VMEM((N_HEAD, rows, 256), BF),
+            pltpu.VMEM((N_HEAD, rows + rows // 2, 128), BF),
+            pltpu.VMEM((N_HEAD, rows + rows // 2, 128), BF),
             pltpu.VMEM((N_HEAD, rows, 256), BF),
             pltpu.VMEM((qkv[1], 256), F32),
             pltpu.VMEM((qkv[1], 256), F32),

time: 242 us -> 240 us (level)
  no operation moved by 1% of the time
where the time goes in v3:
time: 240 us; the launch traced here: 235 us
  Pallas kernels  234 us (98%)
    pallas_call x1, Pallas kernels, front(): pl.pallas_call(front_kernel, out_shape=outs, in_specs=[SM, VM, VM, VM] +...  139 us
    pallas_call x1, Pallas kernels, back(): pl.pallas_call(back_kernel, out_shape=(out((rows, width), BF), out((rows,...  74 us
    pallas_call x1, Pallas kernels, adam(): pl.pallas_call(adam_kernel, out_shape=[out(v.shape, v.dtype) for v in (*m...  20.6 us

profile of v3, /device:TPU:1, one launch (start us, length us, event | category | flops | bytes accessed | tf_op | source)
XLA Modules:
  0.0 235.4 jit_solution(13508130927904882795)
XLA Ops:
  1.3 139.3 %front.1 = (bf16[4,256,768]{2,1,0:T(8,128)(2,1)}, bf16[3,1024,256]{2,1,0:T(8,128)(2,1)}, bf16[768,768]{1,0:T(8,128)(2,1)}, bf16[4,192,768]{2,1,0:T(8,128)(2,1)},...) custom-call(s32[1]{0:T(128)S(6)} %copy.43.length_ref, ...), custom_call_target="tpu_custom_call" | custom-call | flops 142999994368 | bytes 130000000 | tf_op jit(solution)/shard_map/front/pallas_call | solution.py:684
  140.6 74.0 %back.1 = (bf16[256,768]{1,0:T(8,128)(2,1)}, f32[256,768]{1,0:T(8,128)}, bf16[2,768,384]{2,1,0:T(8,128)(2,1)}, f32[40,768]{1,0:T(8,128)}, f32[8,128]{1,0:T(8,128...) custom-call(s32[1]{0:T(128)S(6)} %copy.43.length_ref, f32[4,768]{1,0:T(4,128)} %refs_14_.1, f32[32,768]{1,0:T(8,128)} %bitcast.51, ...), custom_call_target="tpu_custom_call" | custom-call | flops 65999998976 | bytes 60000000 | tf_op jit(solution)/shard_map/back/pallas_call | solution.py:1177
  214.6 20.6 %adamw.1 = (f32[768,768]{1,0:T(8,128)}, f32[768,768]{1,0:T(8,128)}, f32[768,768]{1,0:T(8,128)}, f32[768,768]{1,0:T(8,128)}, f32[768,768]{1,0:T(8,128)}, /*index=...) custom-call(f32[8,128]{1,0:T(8,128)} %get-tuple-element.81.norm, ...), custom_call_target="tpu_custom_call" | custom-call | flops 14300000256 | bytes 13000000 | tf_op jit(solution)/shard_map/adamw/pallas_call | solution.py:1317
